TPU v7x, 256 devices: a whole 4x4x8 slice. The times are simulated.
256 devices in a mesh: feed: 128 (over y_lo, x, z, core), rep: 2 (over y_hi).
Axes of the slice: x: 4, y: 4 (y_hi: 2, y_lo: 2; y = y_hi * 2 + y_lo), z: 8, core: 2. Of those that a mesh axis runs over, the one named last changes fastest.
Arguments:
- voltages: bfloat16 [1024, 262144], P('feed', 'rep'), may hold values from -6 to 6
- pfb_window: float32 [8192], replicated, may hold values from 0.1 to 2
- channel_map: int32 [512], replicated, may hold values from 0 to 511, each once
- beam_layout: int32 [1024], replicated, may hold values from 0 to 1023, each once
Outputs:
- visibilities: bfloat16 [512, 1024, 2, 1024], P('rep', 'feed')
- beam_power: float32 [1024, 512], P('feed')
Inputs may be any that keep to these rules, and one draw needn't show every extreme that they name: `channel_map`: each channel appears once. `beam_layout`: each input appears once.
All inputs are finite; a program needn't handle non-finite values.
Results may differ from a plain program's by a relative error of at most 0.006.
Values may be sent and summed in bfloat16 or wider, within the bound.
No kernel may reach another device: no remote copies, remote signals or barrier semaphores. Data moves between devices by JAX's collectives and lax.ppermute only.
A program may use at most 192 MiB of HBM per device.

v0:
```python
import math

import jax
import jax.numpy as jnp
import numpy as np
from jax import lax
from jax.sharding import PartitionSpec as P

CYL = 4
POS = 128
DFT = 2048
CHANNELS = 512
CH0 = 256
TAPS = 4


def shifted(value, axis, steps):
    count = lax.axis_size(axis)
    first, last = (max(0, -steps), min(count, count - steps))
    return lax.ppermute(value, axis, [(source, source + steps) for source in range(first, last)])


def wave_columns(dft_length, channels, first_bin):
    samples = jnp.arange(dft_length, dtype=jnp.int32)
    freq_bins = jnp.arange(channels, dtype=jnp.int32) + first_bin
    phase_index = samples[:, None] * freq_bins[None, :] % dft_length
    angles = phase_index.astype(jnp.float32) * (2.0 * np.pi / dft_length)
    return jnp.concatenate([jnp.cos(angles), -jnp.sin(angles)], axis=1)


def weight_taps(window_part, wave_table, tap_count, norm_taps, channels):
    dft_length = wave_table.shape[0]
    weighted = (
        window_part.reshape(tap_count, dft_length, 1)
        * wave_table[None]
        / math.sqrt(norm_taps * channels)
    )
    return weighted.astype(jnp.bfloat16)


def position_tables(grid_size):
    places = jnp.arange(grid_size, dtype=jnp.int32)
    phase_index = places[:, None] * places[None, :] % grid_size
    angles = phase_index.astype(jnp.float32) * (2.0 * np.pi / grid_size)
    return jnp.stack([jnp.cos(angles), jnp.sin(angles)]).astype(jnp.bfloat16)


def quarter_tables(cylinders):
    quarter_turns = np.arange(cylinders)[:, None] * np.arange(cylinders)[None, :] % 4
    real_table = np.array([1.0, 0.0, -1.0, 0.0])[quarter_turns]
    imag_table = np.array([0.0, -1.0, 0.0, 1.0])[quarter_turns]
    return (jnp.asarray(real_table, jnp.float32), jnp.asarray(imag_table, jnp.float32))


def beam_intensity(cell_grid, beam_tables, turn_real, turn_imag, beam_scale):
    highest = lax.Precision.HIGHEST
    mixed = jnp.einsum(
        "anp,cpqf->ancqf", beam_tables, cell_grid, preferred_element_type=jnp.float32
    )
    north_real = mixed[0, :, :, 0] + mixed[1, :, :, 1]
    north_imag = mixed[0, :, :, 1] - mixed[1, :, :, 0]
    east_real = jnp.einsum("ec,ncf->enf", turn_real, north_real, precision=highest) - jnp.einsum(
        "ec,ncf->enf", turn_imag, north_imag, precision=highest
    )
    east_imag = jnp.einsum("ec,ncf->enf", turn_imag, north_real, precision=highest) + jnp.einsum(
        "ec,ncf->enf", turn_real, north_imag, precision=highest
    )
    return jnp.sum(east_real * east_real + east_imag * east_imag, axis=2).reshape(-1) * beam_scale


def gram_rows(row_data, col_data):
    real_part = jnp.einsum("rqf,bqf->rb", row_data, col_data, preferred_element_type=jnp.float32)
    imag_part = jnp.einsum(
        "rf,bf->rb", row_data[:, 1], col_data[:, 0], preferred_element_type=jnp.float32
    ) - jnp.einsum("rf,bf->rb", row_data[:, 0], col_data[:, 1], preferred_element_type=jnp.float32)
    return jnp.stack([real_part, imag_part], axis=1)


def on_device(voltages, pfb_window, channel_map, beam_layout):
    feed_count = lax.axis_size("feed")
    rep_count = lax.axis_size("rep")
    inp_dev, own_samples = voltages.shape
    dft_length = DFT
    frames = own_samples // dft_length
    total_frames = frames * rep_count
    inputs = inp_dev * feed_count
    slot_count = 2 * CHANNELS
    per_dev = slot_count // feed_count
    half_rows = inputs // 2
    rows_rep = half_rows // rep_count
    wave_table = wave_columns(dft_length, CHANNELS, CH0)
    margin = shifted(voltages[:, own_samples - (TAPS - 1) * dft_length :], "rep", 1)
    sample_blocks = jnp.concatenate([margin, voltages], axis=1).reshape(
        inp_dev, frames + TAPS - 1, dft_length
    )
    spectra = jnp.zeros((inp_dev, slot_count, frames), jnp.float32)
    for tap_index in range(TAPS):
        tap_table = weight_taps(
            pfb_window[tap_index * dft_length : (tap_index + 1) * dft_length],
            wave_table,
            1,
            TAPS,
            CHANNELS,
        )[0]
        spectra = spectra + jnp.einsum(
            "ifk,km->imf",
            sample_blocks[:, tap_index : tap_index + frames],
            tap_table,
            preferred_element_type=jnp.float32,
        )
    spectra = spectra.astype(jnp.bfloat16)
    picked_columns = jnp.stack([channel_map, channel_map + CHANNELS], axis=1).reshape(-1)
    chosen = jnp.take(spectra, picked_columns, axis=1)
    outgoing = jnp.broadcast_to(
        chosen.reshape(inp_dev, CHANNELS, 1, 2, frames), (inp_dev, CHANNELS, 2, 2, frames)
    ).reshape(inp_dev, slot_count, 2, frames)
    columns = lax.all_to_all(outgoing, "feed", split_axis=1, concat_axis=0, tiled=True)
    first_slot = lax.axis_index("feed") * per_dev
    halves = [(first_slot + slot_index) % 2 for slot_index in range(per_dev)]
    beam_tables = position_tables(POS)
    turn_real, turn_imag = quarter_tables(CYL)
    beam_scale = 1.0 / (total_frames * CYL * POS)
    powers = []
    for slot_index in range(per_dev):
        row_order = lax.dynamic_slice_in_dim(
            beam_layout, halves[slot_index] * (CYL * POS), CYL * POS
        )
        cell_grid = jnp.take(columns[:, slot_index], row_order, axis=0).reshape(CYL, POS, 2, frames)
        powers.append(beam_intensity(cell_grid, beam_tables, turn_real, turn_imag, beam_scale))
    beam_power = lax.psum(jnp.stack(powers), "rep")
    rep_index = lax.axis_index("rep")
    arriving = lax.all_gather(columns, "rep", axis=3, tiled=True)
    pieces = []
    for slot_index in range(per_dev):
        slot_data = arriving[:, slot_index]
        row_data = lax.dynamic_slice_in_dim(
            slot_data, halves[slot_index] * half_rows + rep_index * rows_rep, rows_rep, 0
        )
        pieces.append(gram_rows(row_data, slot_data))
    summed = jnp.stack(pieces, axis=1)
    visibilities = (summed / total_frames).astype(jnp.bfloat16)
    return (visibilities, beam_power)


def solution(mesh):
    return jax.shard_map(
        on_device,
        mesh=mesh,
        in_specs=(P("feed", "rep"), P(), P(), P()),
        out_specs=(P("rep", "feed", None, None), P("feed", None)),
        check_vma=False,
    )
```

profile of v0, /device:TPU:1, one launch (start us, length us, event | category | flops | bytes accessed | tf_op | source)
XLA Modules:
  0.0 378.9 jit_solution(6268097476101541348)
XLA Ops:
  8.1 5.6 %collective-permute-start = (bf16[8,6144]{1,0:T(8,128)(2,1)S(1)}, bf16[8,6144]{1,0:T(8,128)(2,1)S(1)}, u32[]{:S(2)}, u32[]{:S(2)}) collective-permute-start(bf16[8,6144]{1,0:T(8,128)(2,1)S(1)} %slice.268), channel_id=1, source_target_pairs={{0,1},{2,3},{4,5},{6,7},{8,9},{10,11},{12,13},{14,15},{16,17},{18,... | collective-permute-start | bytes 294920 | tf_op jit(solution)/shard_map/ppermute | solution.py:20
  14.5 18.0 %fusion.38 = (f32[2048,512]{1,0:T(8,128)}, f32[2048,512]{1,0:T(8,128)}) fusion(s32[512]{0:T(512)S(1)} %iota_add_fusion), kind=kLoop, calls=%fused_computation.64 | loop fusion | flops 15728640 | bytes 8390656 | tf_op jit(solution)/shard_map/cos | solution.py:28
  37.4 3.3 fusion.10
  40.6 3.3 fusion.4
  43.9 3.3 fusion.7
  47.2 3.6 fusion.43
  52.5 7.6 %gather_fusion = bf16[1024,8,64]{2,1,0:T(8,128)(2,1)} fusion(bf16[8,1024,64]{2,0,1:T(8,128)(2,1)S(1)} %copy.114, s32[1024]{0:T(1024)S(1)} %broadcast_clamp_fusion), kind=kCustom, calls=%fused_computation.8 | custom fusion | bytes 2101248 | tf_op jit(solution)/shard_map/jit(_take)/gather | solution.py:113
  60.1 5.3 %broadcast_select_fusion = bf16[8,512,2,64]{3,0,2,1:T(8,128)(2,1)S(1)} fusion(bf16[8,512,2,64]{3,0,2,1:T(8,128)(2,1)} %bitcast.406, pred[512,2]{1,0:T(8,128)(4,1)S(1)} %copy.108), kind=kLoop, calls=%fused_computation.65 | loop fusion | flops 524288 | bytes 2098176 | tf_op jit(solution)/shard_map/jit(_take)/select_n | solution.py:113
  67.5 4.2 %broadcast_in_dim.34 = bf16[8,512,2,2,64]{4,3,0,2,1:T(2,128)(2,1)} broadcast(bf16[8,512,2,64]{3,2,0,1:T(2,128)(2,1)S(1)} %copy.115), dimensions={0,1,3,4} | broadcast | bytes 3145728 | tf_op jit(solution)/shard_map/broadcast_in_dim | solution.py:114
  71.7 9.8 %reshape.491 = bf16[128,2,4096]{2,1,0:T(2,128)(2,1)} reshape(bf16[1024,8,2,64]{3,2,1,0:T(2,128)(2,1)} %bitcast.403) | data formatting | bytes 4194304
  81.5 13.3 %all-to-all-start = ((bf16[128,2,4096]{2,1,0:T(2,128)(2,1)}), bf16[128,2,4096]{2,1,0:T(2,128)(2,1)S(1)}, u32[]{:S(2)}, u32[]{:S(2)}) async-start(bf16[128,2,4096]{2,1,0:T(2,128)(2,1)} %reshape.491), calls=%async_computation | async-start | bytes 4194304 | tf_op jit(solution)/shard_map/all_to_all | solution.py:117
  95.5 50.2 %all-to-all-done = bf16[128,2,4096]{2,1,0:T(2,128)(2,1)S(1)} async-done(((bf16[128,2,4096]{2,1,0:T(2,128)(2,1)}), bf16[128,2,4096]{2,1,0:T(2,128)(2,1)S(1)}, u32[]{:S(2)}, u32[]{:S(2)}) %all-to-all-start) | async-done | bytes 2097184 | tf_op jit(solution)/shard_map/all_to_all | solution.py:117
  145.7 4.5 %reshape.492 = bf16[1024,8,2,64]{3,2,1,0:T(2,128)(2,1)} reshape(bf16[128,2,4096]{2,1,0:T(2,128)(2,1)S(1)} %all-to-all-done) | data formatting | bytes 4194304
  150.2 3.3 copy.258
  153.5 6.3 %copy.117 = bf16[128,8,8,2,64]{4,3,1,0,2:T(2,128)(2,1)} copy(bf16[128,8,8,2,64]{4,2,0,3,1:T(8,128)(2,1)S(1)} %bitcast.405) | data formatting | bytes 4194304 | tf_op jit(solution)/shard_map/all_to_all | solution.py:117
  159.8 7.5 %copy.118 = bf16[1024,8,2,64]{0,1,2,3:T(8,128)(2,1)} copy(bf16[1024,8,2,64]{3,2,0,1:T(2,128)(2,1)} %bitcast.401) | data formatting | bytes 4194304 | tf_op jit(solution)/shard_map/all_to_all | solution.py:117
  167.3 5.3 %slice_bitcast_fusion = (bf16[1024,2,64]{2,1,0:T(2,128)(2,1)S(1)}, bf16[1024,2,64]{2,1,0:T(2,128)(2,1)S(1)}, bf16[1024,2,64]{2,1,0:T(2,128)(2,1)S(1)}, bf16[1024...) fusion(bf16[1024,8,2,64]{3,2,0,1:T(2,128)(2,1)} %bitcast.402), kind=kLoop, calls=%fused_computation.139 | loop fusion | bytes 4194304 | tf_op jit(solution)/shard_map/squeeze | solution.py:128
  172.6 3.1 gather_fusion.1
  175.7 2.9 broadcast_select_fusion.8
  182.7 3.1 gather_fusion.2
  185.8 3.7 broadcast_select_fusion.7
  195.4 2.9 broadcast_select_fusion.6
  203.3 2.9 broadcast_select_fusion.5
  239.9 8.4 %psum.7 = f32[8,512]{1,0:T(8,128)} all-reduce(f32[8,512]{1,0:T(8,128)S(1)} %stack.162), channel_id=1, replica_groups=mesh['feed'=128,'rep'=2] {'rep'}, use_global_device_ids=true, to_apply=%region_8.10 | all-reduce | flops 4096 | bytes 32768 | tf_op jit(solution)/shard_map/psum | solution.py:130
  248.3 33.0 %all-gather.2.cloned.1.call-done = bf16[1024,8,2,128]{0,1,2,3:T(8,128)(2,1)} async-done(((bf16[1024,8,2,64]{0,1,2,3:T(8,128)(2,1)}), bf16[1024,8,2,128]{0,1,2,3:T(8,128)(2,1)}) %all-gather.2.cloned.1.call-update) | async-done | bytes 4194320 | tf_op jit(solution)/shard_map/all_gather | solution.py:132
  281.3 23.5 %fusion.198 = (bf16[1024,1,2,128]{0,1,2,3:T(2,128)(2,1)S(1)}, bf16[1024,1,2,128]{0,1,2,3:T(2,128)(2,1)S(1)}, bf16[1024,1,2,128]{0,1,2,3:T(2,128)(2,1)}, bf16[102...) fusion(bf16[1024,8,2,128]{0,1,2,3:T(8,128)(2,1)} %all-gather.2., ...), kind=kLoop, calls=%fused_computation.366 | loop fusion | bytes 8388608 | tf_op jit(solution)/shard_map/slice | solution.py:135
  304.8 2.4 copy.173
  310.2 2.4 copy.174
  315.5 2.4 copy.175
  321.0 2.4 copy.176
  326.3 2.4 copy.177
  351.0 20.5 %copy.167 = bf16[256,8,2,1024]{3,2,1,0:T(2,128)(2,1)} copy(bf16[256,8,2,1024]{3,0,2,1:T(8,128)(2,1)S(1)} %multiply_convert_fusion) | data formatting | bytes 16777216
  (209 shorter events, 92.6 us)
Async XLA Ops:
  8.1 25.0 %collective-permute-start = (bf16[8,6144]{1,0:T(8,128)(2,1)S(1)}, bf16[8,6144]{1,0:T(8,128)(2,1)S(1)}, u32[]{:S(2)}, u32[]{:S(2)}) collective-permute-start(bf16[8,6144]{1,0:T(8,128)(2,1)S(1)} %slice.268), channel_id=1, source_target_pairs={{0,1},{2,3},{4,5},{6,7},{8,9},{10,11},{12,13},{14,15},{16,17},{18,... | collective-permute-start | bytes 294920 | tf_op jit(solution)/shard_map/ppermute | solution.py:20
  14.5 18.0 %copy-start.32 = (s32[512]{0:T(512)S(1)}, s32[512]{0:T(512)}, u32[]{:S(2)}) copy-start(s32[512]{0:T(512)} %param.10) | copy-start | bytes 6148
  14.5 18.6 %copy-start.16 = (bf16[8,131072]{1,0:T(8,128)(2,1)S(1)}, bf16[8,131072]{1,0:T(8,128)(2,1)}, u32[]{:S(2)}) copy-start(bf16[8,131072]{1,0:T(8,128)(2,1)} %param.8) | copy-start | bytes 6291460
  33.9 2.2 copy-start
  33.9 3.5 copy-start.1
  71.7 23.3 %copy-start.31 = (s32[1024]{0:T(1024)S(1)}, s32[1024]{0:T(1024)}, u32[]{:S(2)}) copy-start(s32[1024]{0:T(1024)} %param.11) | copy-start | bytes 12292
  81.5 64.2 %all-to-all-start = ((bf16[128,2,4096]{2,1,0:T(2,128)(2,1)}), bf16[128,2,4096]{2,1,0:T(2,128)(2,1)S(1)}, u32[]{:S(2)}, u32[]{:S(2)}) async-start(bf16[128,2,4096]{2,1,0:T(2,128)(2,1)} %reshape.491), calls=%async_computation | async-start | bytes 4194304 | tf_op jit(solution)/shard_map/all_to_all | solution.py:117
  94.8 186.4 %all-gather.2.cloned.1.call-start = ((), (), s32[]{:S(2)}) async-start(), calls=%async_computation.1 | async-start | bytes 6291456 | tf_op jit(solution)/shard_map/all_gather | solution.py:132
  167.3 13.2 %copy-start.17 = (f32[4,4,1]{1,0,2:T(4,128)S(1)}, f32[4,4,1]{1,0,2:T(4,128)}, u32[]{:S(2)}) copy-start(f32[4,4,1]{1,0,2:T(4,128)} %constant.156) | copy-start | bytes 196
  167.3 14.3 %copy-start.18 = (f32[4,4,1]{1,0,2:T(4,128)S(1)}, f32[4,4,1]{1,0,2:T(4,128)}, u32[]{:S(2)}) copy-start(f32[4,4,1]{1,0,2:T(4,128)} %constant.155) | copy-start | bytes 196
  213.1 13.2 %copy-start.20 = (f32[128,64,4]{0,2,1:T(4,128)S(1)}, f32[128,64,4]{0,2,1:T(4,128)}, u32[]{:S(2)}) copy-start(f32[128,64,4]{0,2,1:T(4,128)} %fusion.172) | copy-start | bytes 393220
  214.2 12.5 %copy-start.19 = (f32[128,64,4]{0,2,1:T(4,128)S(1)}, f32[128,64,4]{0,2,1:T(4,128)}, u32[]{:S(2)}) copy-start(f32[128,64,4]{0,2,1:T(4,128)} %fusion.174) | copy-start | bytes 393220
  215.3 11.9 %copy-start.22 = (f32[128,64,4]{0,2,1:T(4,128)S(1)}, f32[128,64,4]{0,2,1:T(4,128)}, u32[]{:S(2)}) copy-start(f32[128,64,4]{0,2,1:T(4,128)} %fusion.166) | copy-start | bytes 393220
  217.4 10.3 %copy-start.21 = (f32[128,64,4]{0,2,1:T(4,128)S(1)}, f32[128,64,4]{0,2,1:T(4,128)}, u32[]{:S(2)}) copy-start(f32[128,64,4]{0,2,1:T(4,128)} %fusion.168) | copy-start | bytes 393220
  219.2 9.0 %copy-start.24 = (f32[128,64,4]{0,2,1:T(4,128)S(1)}, f32[128,64,4]{0,2,1:T(4,128)}, u32[]{:S(2)}) copy-start(f32[128,64,4]{0,2,1:T(4,128)} %fusion.160) | copy-start | bytes 393220
  219.3 9.3 %copy-start.23 = (f32[128,64,4]{0,2,1:T(4,128)S(1)}, f32[128,64,4]{0,2,1:T(4,128)}, u32[]{:S(2)}) copy-start(f32[128,64,4]{0,2,1:T(4,128)} %fusion.162) | copy-start | bytes 393220
  219.3 9.7 %copy-start.26 = (f32[128,64,4]{0,2,1:T(4,128)S(1)}, f32[128,64,4]{0,2,1:T(4,128)}, u32[]{:S(2)}) copy-start(f32[128,64,4]{0,2,1:T(4,128)} %fusion.154) | copy-start | bytes 393220
  219.6 9.9 %copy-start.25 = (f32[128,64,4]{0,2,1:T(4,128)S(1)}, f32[128,64,4]{0,2,1:T(4,128)}, u32[]{:S(2)}) copy-start(f32[128,64,4]{0,2,1:T(4,128)} %fusion.156) | copy-start | bytes 393220
  219.6 10.4 %copy-start.28 = (f32[128,64,4]{0,2,1:T(4,128)S(1)}, f32[128,64,4]{0,2,1:T(4,128)}, u32[]{:S(2)}) copy-start(f32[128,64,4]{0,2,1:T(4,128)} %fusion.148) | copy-start | bytes 393220
  219.6 10.8 %copy-start.27 = (f32[128,64,4]{0,2,1:T(4,128)S(1)}, f32[128,64,4]{0,2,1:T(4,128)}, u32[]{:S(2)}) copy-start(f32[128,64,4]{0,2,1:T(4,128)} %fusion.150) | copy-start | bytes 393220
  225.9 5.0 %copy-start.30 = (f32[128,64,4]{0,2,1:T(4,128)S(1)}, f32[128,64,4]{0,2,1:T(4,128)}, u32[]{:S(2)}) copy-start(f32[128,64,4]{0,2,1:T(4,128)} %fusion.142) | copy-start | bytes 393220
  226.7 8.5 %copy-start.29 = (f32[128,64,4]{0,2,1:T(4,128)S(1)}, f32[128,64,4]{0,2,1:T(4,128)}, u32[]{:S(2)}) copy-start(f32[128,64,4]{0,2,1:T(4,128)} %fusion.144) | copy-start | bytes 393220
  340.9 1.9 copy-start.2
  342.1 1.6 copy-start.10
  343.0 1.4 copy-start.4
  343.0 1.7 copy-start.11
  343.7 1.7 copy-start.12
  344.7 1.4 copy-start.6
  344.7 1.7 copy-start.13
  345.4 1.7 copy-start.14
  346.4 1.4 copy-start.8
  346.4 1.7 copy-start.15
  (4 other events, 5.3 us)
Sparse Core Ops, SparseCore 0:
  221.9 59.2 all-gather.1
where the time goes:
time: 382 us; the launch traced here: 379 us
  local copies, waits for them, and re-layouts  144 us (38%)
  waiting for transfers between devices  83.2 us (22%)
  matrix products  59.3 us (16%)
  other arithmetic  48.9 us (13%)
  starting transfers between devices  19 us (5%)
  between operations  15.7 us (4%)
  blocking collectives  8.42 us (2%)
    unnamed x77, local copies, waits for them, and re-layouts  57.3 us
    all_to_all x1, waiting for transfers between devices, on_device(): lax.all_to_all(outgoing, 'feed', split_axis=1, concat_axis=0, tiled=True)  50.2 us
    all_gather x1, waiting for transfers between devices, on_device(): arriving = lax.all_gather(columns, 'rep', axis=3, tiled=True)  33 us
    slice x1, local copies, waits for them, and re-layouts, on_device(): slot_data = arriving[:, slot_index]  23.5 us
    select_n x8, other arithmetic, on_device(): jnp.take(columns[:, slot_index], row_order, axis=0)  19.8 us
    gather x8, local copies, waits for them, and re-layouts, on_device(): jnp.take(columns[:, slot_index], row_order, axis=0)  19.4 us
    cos x1, other arithmetic, wave_columns(): return jnp.concatenate([jnp.cos(angles), -jnp.sin(angles)], axis=1)  18 us
    all_to_all x3, local copies, waits for them, and re-layouts, on_device(): lax.all_to_all(outgoing, 'feed', split_axis=1, concat_axis=0, tiled=True)  17.1 us
  transfers between devices with their start and end apart: 3, of which 2 were waited for; matrix products, arithmetic and copies ran while one was open for 10% of the time, Pallas kernels for 0%

commit v1 on v0

v1 whole, which is shorter than its diff:
```python
import math

import jax
import jax.numpy as jnp
import numpy as np
from jax import lax
from jax.experimental import pallas as pl
from jax.experimental.pallas import tpu as pltpu
from jax.sharding import PartitionSpec as P

CYL = 4
POS = 128
DFT = 2048
CHANNELS = 512
CH0 = 256
TAPS = 4
HALF = DFT // 2
VMEM = 56 * 1024 * 1024
NT = (((1,), (1,)), ((), ()))


def wave_rows():
    samples = np.arange(HALF)
    rows = []
    for parity in range(2):
        bins = CH0 + np.arange(parity, CHANNELS, 2)
        angles = (bins[:, None] * samples[None, :] % DFT) * (2.0 * np.pi / DFT)
        rows += [np.cos(angles), -np.sin(angles)]
    return np.concatenate(rows).astype(np.float32).astype(jnp.bfloat16)


def order_table(inputs, frames):
    part, frame, feed = np.meshgrid(
        np.arange(2), np.arange(frames), np.arange(inputs), indexing="ij"
    )
    target = ((feed * 2 + part) * frames + frame).reshape(-1)
    table = np.zeros((target.size, target.size), np.float32)
    table[np.arange(target.size), target] = 1.0
    return table.astype(jnp.bfloat16)


def position_tables():
    places = np.arange(POS)
    angles = (places[:, None] * places[None, :] % POS) * (2.0 * np.pi / POS)
    tables = np.concatenate([np.cos(angles), np.sin(angles)])
    return tables.astype(np.float32).astype(jnp.bfloat16)


def filter_kernel(volt, margin, window, waves, order, slots, out, blocks, spectra, sorted_, rows):
    inputs = volt.shape[0]
    frames = volt.shape[1] // DFT
    scale = 1.0 / math.sqrt(TAPS * CHANNELS)

    def taps_of(at):
        return [window[:, pl.ds(t * DFT + at, 128)] * scale for t in range(TAPS)]

    def chunk(j, carry):
        low = pl.multiple_of(j * 128, 128)
        high = pl.multiple_of(j * 128 + HALF, 128)
        sums = []
        for at in (low, high):
            weights = [jnp.broadcast_to(w, (inputs, 128)) for w in taps_of(at)]
            held = [margin[:, pl.ds(t * DFT + at, 128)].astype(jnp.float32) for t in range(3)]
            column = []
            for f in range(frames):
                held.append(volt[:, pl.ds(f * DFT + at, 128)].astype(jnp.float32))
                total = held[0] * weights[0]
                for t in range(1, TAPS):
                    total = total + held[t] * weights[t]
                held = held[1:]
                column.append(total)
            sums.append(column)
        for f in range(0, frames, 2):
            for parity in range(2):
                pair = []
                for g in (f, f + 1):
                    first, second = sums[0][g], sums[1][g]
                    pair.append(first - second if parity else first + second)
                blocks[parity, pl.ds(f * inputs, 2 * inputs), pl.ds(low, 128)] = jnp.concatenate(
                    pair, axis=0
                ).astype(jnp.bfloat16)
        return carry

    lax.fori_loop(0, HALF // 128, chunk, 0)

    columns = inputs * frames
    half_ch = CHANNELS // 2
    for parity in range(2):
        for part in range(2):
            first = (parity * 2 + part) * half_ch
            spectra[parity * half_ch : (parity + 1) * half_ch, part * columns : (part + 1) * columns] = (
                lax.dot_general(
                    waves[first : first + half_ch, :],
                    blocks[parity],
                    NT,
                    preferred_element_type=jnp.float32,
                ).astype(jnp.bfloat16)
            )
    for at in range(0, 2 * columns, 256):
        sorted_[:, at : at + 256] = jnp.dot(
            spectra[...], order[:, at : at + 256], preferred_element_type=jnp.float32
        ).astype(jnp.bfloat16)
    place = lax.broadcasted_iota(jnp.int32, (slots.shape[0], CHANNELS), 1)
    channel = jnp.where(place < half_ch, 2 * place, 2 * (place - half_ch) + 1)
    wide = 2 * frames
    for c in range(slots.shape[1]):
        pick = (channel == slots[:, c : c + 1]).astype(jnp.float32).astype(jnp.bfloat16)
        for pair in range(0, inputs, 2):
            picked = jnp.dot(
                pick,
                sorted_[:, pair * wide : (pair + 2) * wide],
                preferred_element_type=jnp.float32,
            )
            for i in range(2):
                rows[pl.ds(pair + i, slots.shape[0], stride=inputs), :] = picked[
                    :, i * wide : (i + 1) * wide
                ]
        out[:, c * wide : (c + 1) * wide] = rows[...].astype(jnp.bfloat16)


def filtered(volt, margin, window, slots):
    inputs, own = volt.shape
    frames = own // DFT
    dests, chans = slots.shape
    columns = inputs * frames
    return pl.pallas_call(
        filter_kernel,
        out_shape=jax.ShapeDtypeStruct((dests * inputs, chans * 2 * frames), jnp.bfloat16),
        scratch_shapes=[
            pltpu.VMEM((2, columns, HALF), jnp.bfloat16),
            pltpu.VMEM((CHANNELS, 2 * columns), jnp.bfloat16),
            pltpu.VMEM((CHANNELS, 2 * columns), jnp.bfloat16),
            pltpu.VMEM((dests * inputs, 2 * frames), jnp.float32),
        ],
        compiler_params=pltpu.CompilerParams(vmem_limit_bytes=VMEM),
        cost_estimate=pl.CostEstimate(
            flops=2 * columns * CHANNELS * 5 * 1024, bytes_accessed=8 << 20, transcendentals=0
        ),
        name="polyphase",
    )(volt, margin, window, wave_rows(), order_table(inputs, frames), slots)


def beam_kernel(scale, own, layout, tables, out, mixer, mixed):
    inputs = own.shape[0]
    chans = own.shape[1] // 128
    half = CYL * POS
    lane = lax.broadcasted_iota(jnp.int32, (POS, 128), 1)
    first = lane < 64
    collected = jnp.zeros((POS, 128), jnp.float32)
    feed = lax.broadcasted_iota(jnp.int32, (inputs, POS), 0)
    for h in range(2):
        for y in range(CYL):
            at = h * half + y * POS
            hit = (feed == layout[:, at : at + POS]).astype(jnp.float32).astype(jnp.bfloat16)
            mixer[y * 2 * POS : (y + 1) * 2 * POS, :] = lax.dot_general(
                tables[...], hit, NT, preferred_element_type=jnp.float32
            ).astype(jnp.bfloat16)
        mixed[...] = jnp.dot(mixer[...], own[...], preferred_element_type=jnp.float32)

        def turned(value):
            other = pltpu.roll(value, 64, 1)
            return jnp.where(first, other, -other)

        for c in range(chans):
            at = c * 128
            north = []
            for y in range(CYL):
                base = y * 2 * POS
                cosine = mixed[base : base + POS, at : at + 128]
                sine = mixed[base + POS : base + 2 * POS, at : at + 128]
                north.append(cosine + turned(sine))
            even, odd = north[0] + north[2], north[1] + north[3]
            gap, step = north[0] - north[2], turned(north[1] - north[3])
            easts = [even + odd, gap + step, even - odd, gap - step]
            for e, east in enumerate(easts):
                power = jnp.sum(east * east, axis=1, keepdims=True)
                collected = jnp.where(lane == e * 2 * chans + c * 2 + h, power, collected)
    turned_over = collected.T
    for e in range(CYL):
        out[:, e * POS : (e + 1) * POS] = turned_over[e * 2 * chans : (e + 1) * 2 * chans, :] * scale


def beams(own, layout, scale):
    inputs, wide = own.shape
    chans = wide // 128
    return pl.pallas_call(
        lambda *refs: beam_kernel(scale, *refs),
        out_shape=jax.ShapeDtypeStruct((2 * chans, CYL * POS), jnp.float32),
        scratch_shapes=[
            pltpu.VMEM((CYL * 2 * POS, inputs), jnp.bfloat16),
            pltpu.VMEM((CYL * 2 * POS, wide), jnp.float32),
        ],
        compiler_params=pltpu.CompilerParams(vmem_limit_bytes=VMEM),
        cost_estimate=pl.CostEstimate(
            flops=4 * 1024 * inputs * wide, bytes_accessed=4 << 20, transcendentals=0
        ),
        name="beams",
    )(own, layout, position_tables())


def gram_kernel(scale, rep, own, other, beam_own, beam_other, out, beam, rows):
    step = pl.program_id(0)
    count = out.shape[0]
    inputs = own.shape[0]

    @pl.when(step == 0)
    def _():
        beam[...] = beam_own[...] + beam_other[...]

    start = pl.multiple_of((step % 2) * (inputs // 2) + rep[0] * count, count)
    lane = lax.broadcasted_iota(jnp.int32, (count, 128), 1)
    plain, turned = [], []
    for source in (own, other):
        part = source[pl.ds(start, count), :]
        plain.append(part)
        swapped = pltpu.roll(part.astype(jnp.float32), 64, 1)
        turned.append(jnp.where(lane < 64, swapped, -swapped).astype(jnp.bfloat16))
    left = jnp.concatenate(
        [jnp.concatenate(plain, axis=1), jnp.concatenate(turned, axis=1)], axis=0
    )
    for at in range(0, inputs, 256):
        right = jnp.concatenate([own[at : at + 256, :], other[at : at + 256, :]], axis=1)
        products = lax.dot_general(left, right, NT, preferred_element_type=jnp.float32)
        for tile in range(2):
            for part in range(2):
                rows[pl.ds((at // 128 + tile) * 2 + part, count, stride=inputs // 64), :] = products[
                    part * count : (part + 1) * count, tile * 128 : (tile + 1) * 128
                ]
    out[:, 0] = (rows[...] * scale).astype(jnp.bfloat16).reshape(count, inputs // 64, 128)


def gram(rep, own, other, beam_own, beam_other, count, total_frames):
    inputs, wide = own.shape
    slots = 2 * (wide // 128)
    spec = pl.BlockSpec((inputs, 128), lambda s: (0, s // 2))
    small = pl.BlockSpec(beam_own.shape, lambda s: (0, 0))
    return pl.pallas_call(
        lambda *refs: gram_kernel(1.0 / total_frames, *refs),
        grid=(slots,),
        in_specs=[pl.BlockSpec(memory_space=pltpu.SMEM), spec, spec, small, small],
        out_specs=[
            pl.BlockSpec((count, 1, inputs // 64, 128), lambda s: (0, s, 0, 0)),
            small,
        ],
        out_shape=[
            jax.ShapeDtypeStruct((count, slots, inputs // 64, 128), jnp.bfloat16),
            jax.ShapeDtypeStruct(beam_own.shape, jnp.float32),
        ],
        scratch_shapes=[pltpu.VMEM((count * (inputs // 64), 128), jnp.float32)],
        compiler_params=pltpu.CompilerParams(vmem_limit_bytes=VMEM),
        cost_estimate=pl.CostEstimate(
            flops=4 * slots * count * inputs * 256, bytes_accessed=12 << 20, transcendentals=0
        ),
        name="gram",
    )(rep, own, other, beam_own, beam_other)


def on_device(voltages, pfb_window, channel_map, beam_layout):
    feed_count = lax.axis_size("feed")
    rep_count = lax.axis_size("rep")
    inp_dev, own_samples = voltages.shape
    total_frames = own_samples // DFT * rep_count
    inputs = inp_dev * feed_count
    swap = [(0, 1), (1, 0)]
    margin = lax.ppermute(voltages[:, own_samples - (TAPS - 1) * DFT :], "rep", [(0, 1)])
    outgoing = filtered(
        voltages, margin, pfb_window.reshape(1, -1), channel_map.reshape(feed_count, -1)
    )
    own = lax.all_to_all(outgoing, "feed", split_axis=0, concat_axis=0, tiled=True)
    other = lax.ppermute(own, "rep", swap)
    beam_own = beams(own, beam_layout.reshape(1, -1), 1.0 / (total_frames * CYL * POS))
    beam_other = lax.ppermute(beam_own, "rep", swap)
    rep = lax.axis_index("rep").reshape(1)
    count = inputs // 2 // rep_count
    summed, beam_power = gram(rep, own, other, beam_own, beam_other, count, total_frames)
    tiles = inputs // 128
    visibilities = summed.reshape(count, -1, tiles, 2, 128).transpose(0, 1, 3, 2, 4)
    return visibilities.reshape(count, -1, 2, inputs), beam_power


def solution(mesh):
    return jax.shard_map(
        on_device,
        mesh=mesh,
        in_specs=(P("feed", "rep"), P(), P(), P()),
        out_specs=(P("rep", "feed", None, None), P("feed", None)),
        check_vma=False,
    )
```

time: 382 us -> 101 us (0.26)
  local copies, waits for them, and re-layouts: 144 us -> 3.98 us
  waiting for transfers between devices: 83.2 us -> 15.9 us
  matrix products: 59.3 us -> 0 us
  other arithmetic: 48.9 us -> 0 us
  blocking collectives: 8.42 us -> 42.7 us
  Pallas kernels: 0 us -> 25.8 us
  between operations: 15.7 us -> 0.65 us
  starting transfers between devices: 19 us -> 10.8 us
    dot_general x68 -> x0, matrix products: 59.3 us -> none  [the longest x4 13.4 us: on_device(): jnp.einsum('ifk,km->imf', sample_blocks[:, tap_index:tap_index + frames],...]
    unnamed x77 -> x8, local copies, waits for them, and re-layouts: 57.3 us -> 1.67 us
    all_to_all x1 -> x0, waiting for transfers between devices: 50.2 us -> none  [on_device(): lax.all_to_all(outgoing, 'feed', split_axis=1, concat_axis=0, tiled=True)]
    all_to_all x0 -> x1, blocking collectives: none -> 42.7 us  [on_device(): lax.all_to_all(outgoing, 'feed', split_axis=0, concat_axis=0, tiled=True)]
    all_gather x1 -> x0, waiting for transfers between devices: 33 us -> none  [on_device(): arriving = lax.all_gather(columns, 'rep', axis=3, tiled=True)]
    gather x9 -> x0, local copies, waits for them, and re-layouts: 26.9 us -> none  [the longest x8 19.4 us: on_device(): jnp.take(columns[:, slot_index], row_order, axis=0)]
    pallas_call x0 -> x3, Pallas kernels: none -> 25.8 us  [the longest x1 11.2 us: gram(): pl.pallas_call(lambda *refs: gram_kernel(1.0 / total_frames, *refs), grid...]
    slice x4 -> x1, local copies, waits for them, and re-layouts: 26.3 us -> 0.9 us  [on_device(): voltages[:, own_samples - (TAPS - 1) * DFT:]]
  transfers between devices with their start and end apart: 3 -> 3, of which waited for: 2 -> 2; matrix products, arithmetic and copies ran while one was open for 10% -> 1% of each run, Pallas kernels for 0% -> 6%
where the time goes in v1:
time: 101 us; the launch traced here: 99.9 us
  blocking collectives  42.7 us (42%)
  Pallas kernels  25.8 us (26%)
  waiting for transfers between devices  15.9 us (16%)
  starting transfers between devices  10.8 us (11%)
  local copies, waits for them, and re-layouts  3.98 us (4%)
    all_to_all x1, blocking collectives, on_device(): lax.all_to_all(outgoing, 'feed', split_axis=0, concat_axis=0, tiled=True)  42.7 us
    ppermute x1, waiting for transfers between devices, on_device(): beam_other = lax.ppermute(beam_own, 'rep', swap)  15.7 us
    pallas_call x1, Pallas kernels, gram(): pl.pallas_call(lambda *refs: gram_kernel(1.0 / total_frames, *refs), grid...  11.2 us
    pallas_call x1, Pallas kernels, filtered(): pl.pallas_call(filter_kernel, out_shape=jax.ShapeDtypeStruct((dests * inp...  8.55 us
    pallas_call x1, Pallas kernels, beams(): pl.pallas_call(lambda *refs: beam_kernel(scale, *refs), out_shape=jax.Sha...  5.97 us
    ppermute x1, starting transfers between devices, on_device(): lax.ppermute(voltages[:, own_samples - (TAPS - 1) * DFT:], 'rep', [(0, 1)])  5.64 us
    ppermute x1, starting transfers between devices, on_device(): other = lax.ppermute(own, 'rep', swap)  4.24 us
  transfers between devices with their start and end apart: 3, of which 2 were waited for; matrix products, arithmetic and copies ran while one was open for 1% of the time, Pallas kernels for 6%

profile of v1, /device:TPU:1, one launch (start us, length us, event | category | flops | bytes accessed | tf_op | source)
XLA Modules:
  0.0 99.9 jit_solution(2797064064070430774)
XLA Ops:
  0.6 0.9 slice.3
  1.5 5.6 %collective-permute-start = (bf16[8,6144]{1,0:T(8,128)(2,1)S(1)}, bf16[8,6144]{1,0:T(8,128)(2,1)S(1)}, u32[]{:S(2)}, u32[]{:S(2)}) collective-permute-start(bf16[8,6144]{1,0:T(8,128)(2,1)S(1)} %slice.3), channel_id=1, source_target_pairs={{0,1},{2,3},{4,5},{6,7},{8,9},{10,11},{12,13},{14,15},{16,17},{18,... | collective-permute-start | bytes 294920 | tf_op jit(solution)/shard_map/ppermute | solution.py:265
  7.2 1.4 %reshape.26.slots = s32[128,4]{1,0:T(8,128)} reshape(s32[512]{0:T(512)} %param.9) | data formatting | bytes 4096 | tf_op jit(solution)/shard_map/reshape | solution.py:267
  8.6 0.2 collective-permute-done.margin
  8.8 0.0 copy-start.2
  8.8 0.6 copy-done.2
  9.4 8.5 %polyphase.1 = bf16[1024,512]{1,0:T(8,128)(2,1)} custom-call(bf16[8,131072]{1,0:T(8,128)(2,1)} %volt.1, bf16[8,6144]{1,0:T(8,128)(2,1)} %copy-done.2, f32[1,8192]{1,0:T(1,128)} %bitcast.14, bf16[1024,1024]{1,0:T(8,128)(2,1)} %constant.10.clone.waves, bf16[1024,1024]{1,0:T(8,128)(2,1)} %constant.11.clone.order, s32[128,4]{1,0:T(8,128)} %reshape.26.slots), custom_call_target="tpu_custom_call" | custom-call | flops 2684354560 | bytes 8388608 | tf_op jit(solution)/shard_map/polyphase/pallas_call | solution.py:126
  18.0 42.7 %all_to_all.11 = bf16[128,8,512]{2,1,0:T(8,128)(2,1)S(1)} all-to-all(bf16[128,8,512]{2,1,0:T(8,128)(2,1)} %bitcast.13), channel_id=1, replica_groups=mesh['feed'=128,'rep'=2] {'feed'}, dimensions={0} | all-to-all | bytes 2097152 | tf_op jit(solution)/shard_map/all_to_all | solution.py:269
  60.7 0.0 copy-start
  60.7 4.2 %collective-permute-start.1 = (bf16[1024,512]{1,0:T(8,128)(2,1)S(1)}, bf16[1024,512]{1,0:T(8,128)(2,1)S(1)}, u32[]{:S(2)}, u32[]{:S(2)}) collective-permute-start(bf16[1024,512]{1,0:T(8,128)(2,1)S(1)} %bitcast.10), channel_id=1, source_target_pairs={{0,1},{1,0},{2,3},{3,2},{4,5},{5,4},{6,7},{7,6},{8,9},{9,8},{10,11... | collective-permute-start | bytes 3145736 | tf_op jit(solution)/shard_map/ppermute | solution.py:270
  64.9 0.0 copy-done
  64.9 6.0 %beams.1.refs_3_ = f32[8,512]{1,0:T(8,128)} custom-call(bf16[1024,512]{1,0:T(8,128)(2,1)} %bitcast.11, s32[1,1024]{1,0:T(1,128)} %bitcast.15, bf16[256,128]{1,0:T(8,128)(2,1)} %constant.12.clone.refs_2_), custom_call_target="tpu_custom_call" | custom-call | flops 2147483648 | bytes 4194304 | tf_op jit(solution)/shard_map/beams/pallas_call | solution.py:186
  70.9 1.0 collective-permute-start.2
  71.8 15.7 %collective-permute-done.2.refs_4_ = f32[8,512]{1,0:T(8,128)S(1)} collective-permute-done((f32[8,512]{1,0:T(8,128)}, f32[8,512]{1,0:T(8,128)S(1)}, u32[]{:S(2)}, u32[]{:S(2)}) %collective-permute-start.2) | collective-permute-done | bytes 16416 | tf_op jit(solution)/shard_map/ppermute | solution.py:272
  87.6 0.0 copy-start.3
  87.6 0.0 collective-permute-done.1.refs_2_
  87.6 0.0 copy-start.1
  87.6 0.6 copy-done.3
  88.2 0.4 copy-done.1
  88.6 11.2 %gram.1 = (bf16[256,8,16,128]{3,2,1,0:T(8,128)(2,1)}, f32[8,512]{1,0:T(8,128)}) custom-call(s32[1]{0:T(128)} %bitcast.refs_0_, bf16[1024,512]{1,0:T(8,128)(2,1)} %bitcast.12, bf16[1024,512]{1,0:T(8,128)(2,1)} %copy-done.1, f32[8,512]{1,0:T(8,128)} %beams.1.refs_3_, f32[8,512]{1,0:T(8,128)} %copy-done.3), custom_call_target="tpu_custom_call" | custom-call | flops 2147483648 | bytes 12582912 | tf_op jit(solution)/shard_map/gram/pallas_call | solution.py:237
Async XLA Ops:
  1.5 7.3 %collective-permute-start = (bf16[8,6144]{1,0:T(8,128)(2,1)S(1)}, bf16[8,6144]{1,0:T(8,128)(2,1)S(1)}, u32[]{:S(2)}, u32[]{:S(2)}) collective-permute-start(bf16[8,6144]{1,0:T(8,128)(2,1)S(1)} %slice.3), channel_id=1, source_target_pairs={{0,1},{2,3},{4,5},{6,7},{8,9},{10,11},{12,13},{14,15},{16,17},{18,... | collective-permute-start | bytes 294920 | tf_op jit(solution)/shard_map/ppermute | solution.py:265
  8.8 0.6 copy-start.2
  60.7 4.2 %copy-start = (bf16[128,8,512]{2,1,0:T(8,128)(2,1)}, bf16[128,8,512]{2,1,0:T(8,128)(2,1)S(1)}, u32[]{:S(2)}) copy-start(bf16[128,8,512]{2,1,0:T(8,128)(2,1)S(1)} %all_to_all.11) | copy-start | bytes 3145732
  60.7 26.9 %collective-permute-start.1 = (bf16[1024,512]{1,0:T(8,128)(2,1)S(1)}, bf16[1024,512]{1,0:T(8,128)(2,1)S(1)}, u32[]{:S(2)}, u32[]{:S(2)}) collective-permute-start(bf16[1024,512]{1,0:T(8,128)(2,1)S(1)} %bitcast.10), channel_id=1, source_target_pairs={{0,1},{1,0},{2,3},{3,2},{4,5},{5,4},{6,7},{7,6},{8,9},{9,8},{10,11... | collective-permute-start | bytes 3145736 | tf_op jit(solution)/shard_map/ppermute | solution.py:270
  70.9 16.7 %collective-permute-start.2 = (f32[8,512]{1,0:T(8,128)}, f32[8,512]{1,0:T(8,128)S(1)}, u32[]{:S(2)}, u32[]{:S(2)}) collective-permute-start(f32[8,512]{1,0:T(8,128)} %beams.1.refs_3_), channel_id=1, source_target_pairs={{0,1},{1,0},{2,3},{3,2},{4,5},{5,4},{6,7},{7,6},{8,9},{9,8},{10,11... | collective-permute-start | bytes 49160 | tf_op jit(solution)/shard_map/ppermute | solution.py:272
  87.6 0.6 copy-start.3
  87.6 1.0 %copy-start.1 = (bf16[1024,512]{1,0:T(8,128)(2,1)}, bf16[1024,512]{1,0:T(8,128)(2,1)S(1)}, u32[]{:S(2)}) copy-start(bf16[1024,512]{1,0:T(8,128)(2,1)S(1)} %collective-permute-done.1.refs_2_) | copy-start | bytes 3145732

commit v2 on v1

v2 whole, which is shorter than its diff:
```python
import math

import jax
import jax.numpy as jnp
import numpy as np
from jax import lax
from jax.experimental import pallas as pl
from jax.experimental.pallas import tpu as pltpu
from jax.sharding import PartitionSpec as P

CYL = 4
POS = 128
DFT = 2048
CHANNELS = 512
CH0 = 256
TAPS = 4
HALF = DFT // 2
VMEM = 24 * 1024 * 1024
GROUPS = 4
PARTS = (2, 1, 1)
NT = (((1,), (1,)), ((), ()))


def wave_columns():
    samples = np.arange(HALF)
    tables = []
    for parity in range(2):
        bins = CH0 + np.arange(parity, CHANNELS, 2)
        angles = (samples[:, None] * bins[None, :] % DFT) * (2.0 * np.pi / DFT)
        tables.append(np.concatenate([np.cos(angles), -np.sin(angles)], axis=1))
    return np.stack(tables).astype(np.float32).astype(jnp.bfloat16)


def order_table(inputs, frames):
    frame, feed = np.meshgrid(np.arange(frames), np.arange(inputs), indexing="ij")
    target = (feed * frames + frame).reshape(-1)
    table = np.zeros((target.size, target.size), np.float32)
    table[target, np.arange(target.size)] = 1.0
    return table.astype(jnp.bfloat16)


def position_tables():
    places = np.arange(POS)
    angles = (places[:, None] * places[None, :] % POS) * (2.0 * np.pi / POS)
    tables = np.concatenate([np.cos(angles), np.sin(angles)])
    return tables.astype(np.float32).astype(jnp.bfloat16)


def filter_kernel(
    volt_hbm, margin, window_hbm, waves_hbm, order_hbm, slots_hbm, out,
    volt, window, slots, waves, order, blocks, spectra, sorted_, pick, rows, sems,
):
    inputs = volt.shape[0]
    frames = volt.shape[1] // DFT
    dests = out.shape[0] // inputs
    chans = slots.shape[1] // dests
    scale = 1.0 / math.sqrt(TAPS * CHANNELS)
    group = frames // GROUPS
    span = group * DFT
    copies = [
        pltpu.make_async_copy(
            volt_hbm.at[:, pl.ds(g * span, span)], volt.at[:, pl.ds(g * span, span)], sems.at[g]
        )
        for g in range(GROUPS)
    ]
    for parity in range(2):
        copies.append(
            pltpu.make_async_copy(
                waves_hbm.at[parity], waves.at[parity], sems.at[GROUPS + parity]
            )
        )
    copies.append(pltpu.make_async_copy(order_hbm, order, sems.at[GROUPS + 2]))
    taps_copy = pltpu.make_async_copy(window_hbm, window, sems.at[GROUPS + 3])
    taps_copy.start()
    slots_copy = pltpu.make_async_copy(slots_hbm, slots, sems.at[GROUPS + 4])
    slots_copy.start()
    for copy in copies:
        copy.start()

    half_ch = CHANNELS // 2
    place = lax.broadcasted_iota(jnp.int32, (dests, CHANNELS), 1)
    channel = jnp.where(place < half_ch, 2 * place, 2 * (place - half_ch) + 1)
    dest = lax.broadcasted_iota(jnp.int32, (dests, CHANNELS), 0)
    slots_copy.wait()
    held_by = slots[...].astype(jnp.float32)
    for c in range(chans):
        wanted = jnp.sum(
            jnp.where(place == dest * chans + c, held_by, 0.0), axis=1, keepdims=True
        ).astype(jnp.int32)
        pick[c * dests : (c + 1) * dests, :] = (
            (channel == wanted).astype(jnp.float32).astype(jnp.bfloat16)
        )
    taps_copy.wait()

    def fold(g):
        def chunk(j, carry):
            low = pl.multiple_of(j * 128, 128)
            sums = []
            for at in (low, pl.multiple_of(low + HALF, 128)):
                weights = [
                    jnp.broadcast_to(window[:, pl.ds(t * DFT + at, 128)] * scale, (inputs, 128))
                    for t in range(TAPS)
                ]

                def frame(f):
                    if f < 0:
                        value = margin[:, pl.ds((f + TAPS - 1) * DFT + at, 128)]
                    else:
                        value = volt[:, pl.ds(f * DFT + at, 128)]
                    return value.astype(jnp.float32)

                held = [frame(g * group + t + 1 - TAPS) for t in range(TAPS - 1)]
                column = []
                for f in range(g * group, (g + 1) * group):
                    held.append(frame(f))
                    total = held[0] * weights[0]
                    for t in range(1, TAPS):
                        total = total + held[t] * weights[t]
                    held = held[1:]
                    column.append(total)
                sums.append(column)
            for f in range(0, group, 2):
                for parity in range(2):
                    pair = []
                    for k in (f, f + 1):
                        first, second = sums[0][k], sums[1][k]
                        pair.append(first - second if parity else first + second)
                    at = (g * group + f) * inputs
                    blocks[parity, at : at + 2 * inputs, pl.ds(low, 128)] = jnp.concatenate(
                        pair, axis=0
                    ).astype(jnp.bfloat16)
            return carry

        lax.fori_loop(0, HALF // 128, chunk, 0)

    for g in range(GROUPS):
        copies[g].wait()
        fold(g)

    for parity in range(2):
        copies[GROUPS + parity].wait()
        spectra[:, parity * CHANNELS : (parity + 1) * CHANNELS] = jnp.dot(
            blocks[parity], waves[parity], preferred_element_type=jnp.float32
        ).astype(jnp.bfloat16)
    copies[GROUPS + 2].wait()
    for parity in range(2):
        for part in range(2):
            at = parity * CHANNELS + part * half_ch
            turned = jnp.dot(
                order[...], spectra[:, at : at + half_ch], preferred_element_type=jnp.float32
            ).astype(jnp.bfloat16)
            for i in range(inputs):
                to = (2 * i + part) * frames
                sorted_[to : to + frames, parity * half_ch : (parity + 1) * half_ch] = turned[
                    i * frames : (i + 1) * frames, :
                ]
    wide = 2 * frames
    pitch = inputs + 1
    for pair in range(0, inputs, 2):
        picked = lax.dot_general(
            pick[...],
            sorted_[pair * wide : (pair + 2) * wide, :],
            NT,
            preferred_element_type=jnp.float32,
        )
        for c in range(chans):
            for i in range(2):
                rows[pl.ds(c * dests * pitch + pair + i, dests, stride=pitch), :] = picked[
                    c * dests : (c + 1) * dests, i * wide : (i + 1) * wide
                ]
    for c in range(chans):
        for dest in range(0, dests, 2):
            at = (c * dests + dest) * pitch
            pair = [rows[at + k * pitch : at + k * pitch + inputs, :] for k in range(2)]
            out[dest * inputs : (dest + 2) * inputs, c * wide : (c + 1) * wide] = jnp.concatenate(
                pair, axis=0
            ).astype(jnp.bfloat16)


def filtered(volt, margin, window, slots, dests):
    inputs, own = volt.shape
    frames = own // DFT
    chans = slots.shape[1] // dests
    columns = inputs * frames
    vmem = pl.BlockSpec(memory_space=pltpu.VMEM)
    hbm = pl.BlockSpec(memory_space=pltpu.HBM)
    waves, order = jnp.asarray(wave_columns()), jnp.asarray(order_table(inputs, frames))
    volt, window, waves, order, slots = (
        pltpu.with_memory_space_constraint(array, pltpu.HBM)
        for array in (volt, window, waves, order, slots)
    )
    return pl.pallas_call(
        filter_kernel,
        in_specs=[hbm, vmem, hbm, hbm, hbm, hbm],
        out_specs=vmem,
        out_shape=jax.ShapeDtypeStruct((dests * inputs, chans * 2 * frames), jnp.bfloat16),
        scratch_shapes=[
            pltpu.VMEM(volt.shape, jnp.bfloat16),
            pltpu.VMEM(window.shape, jnp.float32),
            pltpu.VMEM(slots.shape, jnp.int32),
            pltpu.VMEM(waves.shape, jnp.bfloat16),
            pltpu.VMEM(order.shape, jnp.bfloat16),
            pltpu.VMEM((2, columns, HALF), jnp.bfloat16),
            pltpu.VMEM((columns, 2 * CHANNELS), jnp.bfloat16),
            pltpu.VMEM((2 * columns, CHANNELS), jnp.bfloat16),
            pltpu.VMEM((chans * dests, CHANNELS), jnp.bfloat16),
            pltpu.VMEM((chans * dests * (inputs + 1), 2 * frames), jnp.float32),
            pltpu.SemaphoreType.DMA((GROUPS + 5,)),
        ],
        compiler_params=pltpu.CompilerParams(vmem_limit_bytes=VMEM),
        cost_estimate=pl.CostEstimate(
            flops=2 * columns * CHANNELS * 4 * 1024, bytes_accessed=8 << 20, transcendentals=0
        ),
        name="polyphase",
    )(volt, margin, window, waves, order, slots)


def beam_kernel(scale, own, layout, tables, out, mixer, mixed):
    inputs = own.shape[0]
    chans = own.shape[1] // 128
    half = CYL * POS
    lane = lax.broadcasted_iota(jnp.int32, (POS, 128), 1)
    first = lane < 64
    collected = jnp.zeros((POS, 128), jnp.float32)
    feed = lax.broadcasted_iota(jnp.int32, (inputs, POS), 0)
    for h in range(2):
        for y in range(CYL):
            at = h * half + y * POS
            hit = (feed == layout[:, at : at + POS]).astype(jnp.float32).astype(jnp.bfloat16)
            mixer[y * 2 * POS : (y + 1) * 2 * POS, :] = lax.dot_general(
                tables[...], hit, NT, preferred_element_type=jnp.float32
            ).astype(jnp.bfloat16)
        mixed[...] = jnp.dot(mixer[...], own[...], preferred_element_type=jnp.float32)

        def turned(value):
            other = pltpu.roll(value, 64, 1)
            return jnp.where(first, other, -other)

        for c in range(chans):
            at = c * 128
            north = []
            for y in range(CYL):
                base = y * 2 * POS
                cosine = mixed[base : base + POS, at : at + 128]
                sine = mixed[base + POS : base + 2 * POS, at : at + 128]
                north.append(cosine + turned(sine))
            even, odd = north[0] + north[2], north[1] + north[3]
            gap, step = north[0] - north[2], turned(north[1] - north[3])
            easts = [even + odd, gap + step, even - odd, gap - step]
            for e, east in enumerate(easts):
                power = jnp.sum(east * east, axis=1, keepdims=True)
                collected = jnp.where(lane == e * 2 * chans + c * 2 + h, power, collected)
    turned_over = collected.T
    for e in range(CYL):
        out[:, e * POS : (e + 1) * POS] = turned_over[e * 2 * chans : (e + 1) * 2 * chans, :] * scale


def beams(own, layout, scale):
    inputs, wide = own.shape
    chans = wide // 128
    return pl.pallas_call(
        lambda *refs: beam_kernel(scale, *refs),
        out_shape=jax.ShapeDtypeStruct((2 * chans, CYL * POS), jnp.float32),
        scratch_shapes=[
            pltpu.VMEM((CYL * 2 * POS, inputs), jnp.bfloat16),
            pltpu.VMEM((CYL * 2 * POS, wide), jnp.float32),
        ],
        compiler_params=pltpu.CompilerParams(vmem_limit_bytes=VMEM),
        cost_estimate=pl.CostEstimate(
            flops=4 * 1024 * inputs * wide, bytes_accessed=4 << 20, transcendentals=0
        ),
        name="beams",
    )(own, layout, position_tables())


def gram_kernel(scale, rep, own, other, *refs):
    out, rows = refs[-2:]
    if len(refs) > 3:
        beam_own, beam_other, out, beam, rows = refs[-5:]
        beam[...] = beam_own[...] + beam_other[...]
    step = pl.program_id(0)
    count, _, tiles, _ = out.shape
    inputs = own.shape[0]
    pitch = tiles + 1
    start = pl.multiple_of((step % 2) * (inputs // 2) + rep[0] * count, count)
    lane = lax.broadcasted_iota(jnp.int32, (count, 128), 1)
    plain, turned = [], []
    for source in (own, other):
        part = source[pl.ds(start, count), :]
        plain.append(part)
        swapped = pltpu.roll(part.astype(jnp.float32), 64, 1)
        turned.append(jnp.where(lane < 64, swapped, -swapped).astype(jnp.bfloat16))
    left = jnp.concatenate(
        [jnp.concatenate(plain, axis=1), jnp.concatenate(turned, axis=1)], axis=0
    )
    for at in range(0, inputs, 256):
        right = jnp.concatenate([own[at : at + 256, :], other[at : at + 256, :]], axis=1)
        products = lax.dot_general(left, right, NT, preferred_element_type=jnp.float32)
        for tile in range(2):
            for part in range(2):
                rows[pl.ds((at // 128 + tile) * 2 + part, count, stride=pitch), :] = products[
                    part * count : (part + 1) * count, tile * 128 : (tile + 1) * 128
                ]
    for r in range(count):
        out[r, 0] = (rows[r * pitch : r * pitch + tiles, :] * scale).astype(jnp.bfloat16)


def gram(rep, own, other, first, extra, count, total_frames):
    inputs, wide = own.shape
    slots = 2 * (wide // 128)
    steps = 2 * (other.shape[1] // 128)
    tiles = inputs // 64
    ops = [rep, own, other, *extra]
    specs = [
        pl.BlockSpec(memory_space=pltpu.SMEM),
        pl.BlockSpec((inputs, 128), lambda s: (0, first + s // 2)),
        pl.BlockSpec((inputs, 128), lambda s: (0, s // 2)),
    ]
    out_specs = [pl.BlockSpec((count, 1, tiles, 128), lambda s: (0, s + 2 * first, 0, 0))]
    out_shape = [jax.ShapeDtypeStruct((count, slots, tiles, 128), jnp.bfloat16)]
    if extra:
        specs.append(pl.BlockSpec(memory_space=pl.ANY))
    if len(extra) > 1:
        small = pl.BlockSpec(extra[1].shape, lambda s: (0, 0))
        specs += [small, small]
        out_specs.append(small)
        out_shape.append(jax.ShapeDtypeStruct(extra[1].shape, jnp.float32))
    return pl.pallas_call(
        lambda *refs: gram_kernel(1.0 / total_frames, *refs),
        grid=(steps,),
        in_specs=specs,
        out_specs=out_specs,
        out_shape=out_shape,
        scratch_shapes=[pltpu.VMEM((count * (tiles + 1), 128), jnp.float32)],
        input_output_aliases={3: 0} if extra else {},
        compiler_params=pltpu.CompilerParams(vmem_limit_bytes=VMEM),
        cost_estimate=pl.CostEstimate(
            flops=4 * steps * count * inputs * 256, bytes_accessed=steps << 20, transcendentals=0
        ),
        name="gram",
    )(*ops)


def on_device(voltages, pfb_window, channel_map, beam_layout):
    feed_count = lax.axis_size("feed")
    rep_count = lax.axis_size("rep")
    inp_dev, own_samples = voltages.shape
    total_frames = own_samples // DFT * rep_count
    inputs = inp_dev * feed_count
    slots = 2 * CHANNELS // feed_count
    swap = [(0, 1), (1, 0)]
    margin = lax.ppermute(voltages[:, own_samples - (TAPS - 1) * DFT :], "rep", [(0, 1)])
    outgoing = filtered(
        voltages, margin, pfb_window.reshape(1, -1), channel_map.reshape(1, -1), feed_count
    )
    own = lax.all_to_all(outgoing, "feed", split_axis=0, concat_axis=0, tiled=True)
    beam_own = beams(own, beam_layout.reshape(1, -1), 1.0 / (total_frames * CYL * POS))
    others, at = [], 0
    for part in PARTS:
        source = own if at + part < slots // 2 else lax.optimization_barrier((own, beam_own))[0]
        others.append(lax.ppermute(source[:, at * 128 : (at + part) * 128], "rep", swap))
        at += part
    beam_other = lax.ppermute(beam_own, "rep", swap)
    rep = lax.axis_index("rep").reshape(1)
    count = inputs // 2 // rep_count
    held, first = (), 0
    for part, other in zip(PARTS, others):
        if first + part == slots // 2:
            held += (beam_own, beam_other)
        held = tuple(gram(rep, own, other, first, held, count, total_frames))
        first += part
    summed, beam_power = held
    tiles = inputs // 128
    visibilities = summed.reshape(count, slots, tiles, 2, 128).transpose(0, 1, 3, 2, 4)
    return visibilities.reshape(count, slots, 2, inputs), beam_power


def solution(mesh):
    return jax.shard_map(
        on_device,
        mesh=mesh,
        in_specs=(P("feed", "rep"), P(), P(), P()),
        out_specs=(P("rep", "feed", None, None), P("feed", None)),
        check_vma=False,
    )
```

time: 101 us -> 87.3 us (0.86)
  Pallas kernels: 25.8 us -> 18.4 us
  waiting for transfers between devices: 15.9 us -> 10.7 us
  local copies, waits for them, and re-layouts: 3.98 us -> 1.05 us
  starting transfers between devices: 10.8 us -> 13.2 us
    ppermute x1, waiting for transfers between devices: 15.7 us -> 3.72 us  [on_device(): beam_other = lax.ppermute(beam_own, 'rep', swap)]
    ppermute x1 -> x3, waiting for transfers between devices: 0.01 us -> 5.31 us  [on_device(): lax.ppermute(source[:, at * 128:(at + part) * 128], 'rep', swap)]
    ppermute x1 -> x3, starting transfers between devices: 4.24 us -> 7.46 us  [on_device(): lax.ppermute(source[:, at * 128:(at + part) * 128], 'rep', swap)]
    pallas_call x1 -> x3, Pallas kernels: 11.2 us -> 8.4 us  [gram(): pl.pallas_call(lambda *refs: gram_kernel(1.0 / total_frames, *refs), grid...]
    pallas_call x1, Pallas kernels: 8.55 us -> 5.87 us  [filtered(): pl.pallas_call(filter_kernel, in_specs=[hbm, vmem, hbm, hbm, hbm, hbm], o...]
    pallas_call x1, Pallas kernels: 5.97 us -> 4.14 us  [beams(): pl.pallas_call(lambda *refs: beam_kernel(scale, *refs), out_shape=jax.Sha...]
    unnamed x8 -> x4, local copies, waits for them, and re-layouts: 1.67 us -> 0.01 us
    ppermute x1, waiting for transfers between devices: 0.2 us -> 1.62 us  [on_device(): lax.ppermute(voltages[:, own_samples - (TAPS - 1) * DFT:], 'rep', [(0, 1)])]
  transfers between devices with their start and end apart: 3 -> 5, of which waited for: 2 -> 4; matrix products, arithmetic and copies ran while one was open for 1% -> 0% of each run, Pallas kernels for 6% -> 12%
where the time goes in v2:
time: 87.3 us; the launch traced here: 86.5 us
  blocking collectives  42.5 us (49%)
  Pallas kernels  18.4 us (21%)
  starting transfers between devices  13.2 us (15%)
  waiting for transfers between devices  10.7 us (12%)
  local copies, waits for them, and re-layouts  1.05 us (1%)
    all_to_all x1, blocking collectives, on_device(): lax.all_to_all(outgoing, 'feed', split_axis=0, concat_axis=0, tiled=True)  42.5 us
    pallas_call x3, Pallas kernels, gram(): pl.pallas_call(lambda *refs: gram_kernel(1.0 / total_frames, *refs), grid...  8.4 us
    ppermute x3, starting transfers between devices, on_device(): lax.ppermute(source[:, at * 128:(at + part) * 128], 'rep', swap)  7.46 us
    pallas_call x1, Pallas kernels, filtered(): pl.pallas_call(filter_kernel, in_specs=[hbm, vmem, hbm, hbm, hbm, hbm], o...  5.87 us
    ppermute x1, starting transfers between devices, on_device(): lax.ppermute(voltages[:, own_samples - (TAPS - 1) * DFT:], 'rep', [(0, 1)])  5.64 us
    ppermute x3, waiting for transfers between devices, on_device(): lax.ppermute(source[:, at * 128:(at + part) * 128], 'rep', swap)  5.31 us
    pallas_call x1, Pallas kernels, beams(): pl.pallas_call(lambda *refs: beam_kernel(scale, *refs), out_shape=jax.Sha...  4.14 us
    ppermute x1, waiting for transfers between devices, on_device(): beam_other = lax.ppermute(beam_own, 'rep', swap)  3.72 us
  transfers between devices with their start and end apart: 5, of which 4 were waited for; matrix products, arithmetic and copies ran while one was open for 0% of the time, Pallas kernels for 12%

profile of v2, /device:TPU:1, one launch (start us, length us, event | category | flops | bytes accessed | tf_op | source)
XLA Modules:
  0.0 86.5 jit_solution(3248417543473775362)
XLA Ops:
  0.6 0.0 copy-start.1
  0.6 0.0 copy-start
  0.7 0.9 %slice.12 = bf16[8,6144]{1,0:T(8,128)(2,1)S(1)} slice(bf16[8,131072]{1,0:T(8,128)(2,1)} %volt_hbm.1), slice={[0:8], [124928:131072]} | slice | bytes 196608 | tf_op jit(solution)/shard_map/slice | solution.py:352
  1.6 5.6 %collective-permute-start = (bf16[8,6144]{1,0:T(8,128)(2,1)S(1)}, bf16[8,6144]{1,0:T(8,128)(2,1)S(1)}, u32[]{:S(2)}, u32[]{:S(2)}) collective-permute-start(bf16[8,6144]{1,0:T(8,128)(2,1)S(1)} %slice.12), channel_id=1, source_target_pairs={{0,1},{2,3},{4,5},{6,7},{8,9},{10,11},{12,13},{14,15},{16,17},{18,... | collective-permute-start | bytes 294920 | tf_op jit(solution)/shard_map/ppermute | solution.py:352
  7.2 1.6 %collective-permute-done.margin = bf16[8,6144]{1,0:T(8,128)(2,1)S(1)} collective-permute-done((bf16[8,6144]{1,0:T(8,128)(2,1)S(1)}, bf16[8,6144]{1,0:T(8,128)(2,1)S(1)}, u32[]{:S(2)}, u32[]{:S(2)}) %collective-permute-start) | collective-permute-done | bytes 98336 | tf_op jit(solution)/shard_map/ppermute | solution.py:352
  8.9 5.9 %polyphase.1 = bf16[1024,512]{1,0:T(8,128)(2,1)S(1)} custom-call(bf16[8,131072]{1,0:T(8,128)(2,1)} %volt_hbm.1, bf16[8,6144]{1,0:T(8,128)(2,1)S(1)} %collective-permute-done.margin, f32[1,8192]{1,0:T(1,128)} %bitcast.21, bf16[2,1024,512]{2,1,0:T(8,128)(2,1)} %constant.10.clone.waves_hbm, bf16[512,512]{1,0:T(8,128)(2,1)} %constant.11.clone.order_hbm, ...), custom_call_target="tpu_custom_call" | custom-call | flops 2147483648 | bytes 8388608 | tf_op jit(solution)/shard_map/polyphase/pallas_call | solution.py:192
  14.7 42.5 %all_to_all.11 = bf16[128,8,512]{2,1,0:T(8,128)(2,1)S(1)} all-to-all(bf16[128,8,512]{2,1,0:T(8,128)(2,1)S(1)} %bitcast.18), channel_id=1, replica_groups=mesh['feed'=128,'rep'=2] {'feed'}, dimensions={0} | all-to-all | bytes 2097152 | tf_op jit(solution)/shard_map/all_to_all | solution.py:356
  57.3 4.3 %collective-permute-start.3 = (bf16[1024,256]{1,0:T(8,128)(2,1)S(1)}, bf16[1024,256]{1,0:T(8,128)(2,1)S(1)}, u32[]{:S(2)}, u32[]{:S(2)}) collective-permute-start(bf16[1024,256]{1,0:T(8,128)(2,1)S(1)} %slice.17), channel_id=1, source_target_pairs={{0,1},{1,0},{2,3},{3,2},{4,5},{5,4},{6,7},{7,6},{8,9},{9,8},{10,11... | collective-permute-start | bytes 1572872 | tf_op jit(solution)/shard_map/ppermute | solution.py:361
  61.6 0.1 collective-permute-start.2
  61.7 0.0 copy-done.1
  61.7 0.0 copy-done
  61.7 4.1 %beams.1.refs_4_ = f32[8,512]{1,0:T(8,128)S(1)} custom-call(bf16[1024,512]{1,0:T(8,128)(2,1)S(1)} %bitcast.13, s32[1,1024]{1,0:T(1,128)S(1)} %bitcast.19, bf16[256,128]{1,0:T(8,128)(2,1)S(1)} %copy-done.1), custom_call_target="tpu_custom_call" | custom-call | flops 2147483648 | bytes 4194304 | tf_op jit(solution)/shard_map/beams/pallas_call | solution.py:261
  65.9 3.0 %collective-permute-start.1 = (bf16[1024,128]{1,0:T(8,128)(2,1)S(1)}, bf16[1024,128]{1,0:T(8,128)(2,1)S(1)}, u32[]{:S(2)}, u32[]{:S(2)}) collective-permute-start(bf16[1024,128]{1,0:T(8,128)(2,1)S(1)} %slice.13), channel_id=1, source_target_pairs={{0,1},{1,0},{2,3},{3,2},{4,5},{5,4},{6,7},{7,6},{8,9},{9,8},{10,11... | collective-permute-start | bytes 786440 | tf_op jit(solution)/shard_map/ppermute | solution.py:361
  69.0 0.1 collective-permute-start.4
  69.1 3.6 %collective-permute-done.3.refs_2_ = bf16[1024,256]{1,0:T(8,128)(2,1)S(1)} collective-permute-done((bf16[1024,256]{1,0:T(8,128)(2,1)S(1)}, bf16[1024,256]{1,0:T(8,128)(2,1)S(1)}, u32[]{:S(2)}, u32[]{:S(2)}) %collective-permute-start.3) | collective-permute-done | bytes 524320 | tf_op jit(solution)/shard_map/ppermute | solution.py:361
  72.7 3.9 %gram.3.refs_3_ = bf16[256,8,16,128]{3,2,1,0:T(8,128)(2,1)} custom-call(s32[1]{0:T(128)} %bitcast.refs_0_, bf16[1024,512]{1,0:T(8,128)(2,1)S(1)} %bitcast.15, bf16[1024,256]{1,0:T(8,128)(2,1)S(1)} %collective-permute-done.3.refs_2_), custom_call_target="tpu_custom_call" | custom-call | flops 1073741824 | bytes 4194304 | tf_op jit(solution)/shard_map/gram/pallas_call | solution.py:328
  76.6 1.7 %collective-permute-done.2.refs_2_ = bf16[1024,128]{1,0:T(8,128)(2,1)S(1)} collective-permute-done((bf16[1024,128]{1,0:T(8,128)(2,1)S(1)}, bf16[1024,128]{1,0:T(8,128)(2,1)S(1)}, u32[]{:S(2)}, u32[]{:S(2)}) %collective-permute-start.2) | collective-permute-done | bytes 262176 | tf_op jit(solution)/shard_map/ppermute | solution.py:361
  78.3 2.2 %gram.4.refs_3_ = bf16[256,8,16,128]{3,2,1,0:T(8,128)(2,1)} custom-call(s32[1]{0:T(128)} %bitcast.refs_0_, bf16[1024,512]{1,0:T(8,128)(2,1)S(1)} %bitcast.16, bf16[1024,128]{1,0:T(8,128)(2,1)S(1)} %collective-permute-done.2.refs_2_, bf16[256,8,16,128]{3,2,1,0:T(8,128)(2,1)} %gram.3.refs_3_), custom_call_target="tpu_custom_call", output_to_operand_aliasing={{}: (3, {})} | custom-call | flops 536870912 | bytes 2097152 | tf_op jit(solution)/shard_map/gram/pallas_call | solution.py:328
  80.5 3.7 %collective-permute-done.4.refs_5_ = f32[8,512]{1,0:T(8,128)S(1)} collective-permute-done((f32[8,512]{1,0:T(8,128)S(1)}, f32[8,512]{1,0:T(8,128)S(1)}, u32[]{:S(2)}, u32[]{:S(2)}) %collective-permute-start.4) | collective-permute-done | bytes 16416 | tf_op jit(solution)/shard_map/ppermute | solution.py:363
  84.3 0.0 collective-permute-done.1.refs_2_
  84.3 2.2 %gram.5 = (bf16[256,8,16,128]{3,2,1,0:T(8,128)(2,1)}, f32[8,512]{1,0:T(8,128)}) custom-call(s32[1]{0:T(128)} %bitcast.refs_0_, bf16[1024,512]{1,0:T(8,128)(2,1)S(1)} %bitcast.17, bf16[1024,128]{1,0:T(8,128)(2,1)S(1)} %collective-permute-done.1.refs_2_, bf16[256,8,16,128]{3,2,1,0:T(8,128)(2,1)} %gram.4.refs_3_, ...), custom_call_target="tpu_custom_call", output_to_operand_aliasing={{0}: (3, {})} | custom-call | flops 536870912 | bytes 2097152 | tf_op jit(solution)/shard_map/gram/pallas_call | solution.py:328
  (3 shorter events, 0.1 us)
Async XLA Ops:
  0.6 61.1 %copy-start.1 = (bf16[256,128]{1,0:T(8,128)(2,1)S(1)}, bf16[256,128]{1,0:T(8,128)(2,1)}, u32[]{:S(2)}) copy-start(bf16[256,128]{1,0:T(8,128)(2,1)} %constant.12.clone.refs_2_) | copy-start | bytes 196612
  0.6 61.1 %copy-start = (s32[1024]{0:T(1024)S(1)}, s32[1024]{0:T(1024)}, u32[]{:S(2)}) copy-start(s32[1024]{0:T(1024)} %param.10) | copy-start | bytes 12292
  1.6 7.3 %collective-permute-start = (bf16[8,6144]{1,0:T(8,128)(2,1)S(1)}, bf16[8,6144]{1,0:T(8,128)(2,1)S(1)}, u32[]{:S(2)}, u32[]{:S(2)}) collective-permute-start(bf16[8,6144]{1,0:T(8,128)(2,1)S(1)} %slice.12), channel_id=1, source_target_pairs={{0,1},{2,3},{4,5},{6,7},{8,9},{10,11},{12,13},{14,15},{16,17},{18,... | collective-permute-start | bytes 294920 | tf_op jit(solution)/shard_map/ppermute | solution.py:352
  57.3 15.4 %collective-permute-start.3 = (bf16[1024,256]{1,0:T(8,128)(2,1)S(1)}, bf16[1024,256]{1,0:T(8,128)(2,1)S(1)}, u32[]{:S(2)}, u32[]{:S(2)}) collective-permute-start(bf16[1024,256]{1,0:T(8,128)(2,1)S(1)} %slice.17), channel_id=1, source_target_pairs={{0,1},{1,0},{2,3},{3,2},{4,5},{5,4},{6,7},{7,6},{8,9},{9,8},{10,11... | collective-permute-start | bytes 1572872 | tf_op jit(solution)/shard_map/ppermute | solution.py:361
  61.6 16.7 %collective-permute-start.2 = (bf16[1024,128]{1,0:T(8,128)(2,1)S(1)}, bf16[1024,128]{1,0:T(8,128)(2,1)S(1)}, u32[]{:S(2)}, u32[]{:S(2)}) collective-permute-start(bf16[1024,128]{1,0:T(8,128)(2,1)S(1)} %slice.16), channel_id=1, source_target_pairs={{0,1},{1,0},{2,3},{3,2},{4,5},{5,4},{6,7},{7,6},{8,9},{9,8},{10,11... | collective-permute-start | bytes 786440 | tf_op jit(solution)/shard_map/ppermute | solution.py:361
  65.9 18.3 %collective-permute-start.1 = (bf16[1024,128]{1,0:T(8,128)(2,1)S(1)}, bf16[1024,128]{1,0:T(8,128)(2,1)S(1)}, u32[]{:S(2)}, u32[]{:S(2)}) collective-permute-start(bf16[1024,128]{1,0:T(8,128)(2,1)S(1)} %slice.13), channel_id=1, source_target_pairs={{0,1},{1,0},{2,3},{3,2},{4,5},{5,4},{6,7},{7,6},{8,9},{9,8},{10,11... | collective-permute-start | bytes 786440 | tf_op jit(solution)/shard_map/ppermute | solution.py:361
  69.0 15.3 %collective-permute-start.4 = (f32[8,512]{1,0:T(8,128)S(1)}, f32[8,512]{1,0:T(8,128)S(1)}, u32[]{:S(2)}, u32[]{:S(2)}) collective-permute-start(f32[8,512]{1,0:T(8,128)S(1)} %beams.1.refs_4_), channel_id=1, source_target_pairs={{0,1},{1,0},{2,3},{3,2},{4,5},{5,4},{6,7},{7,6},{8,9},{9,8},{10,11... | collective-permute-start | bytes 49160 | tf_op jit(solution)/shard_map/ppermute | solution.py:363

commit v3 on v2

--- a/solution.py
+++ b/solution.py
@@ -17,6 +17,7 @@
 HALF = DFT // 2
 VMEM = 24 * 1024 * 1024
 GROUPS = 4
+HEAD = 4
 PARTS = (2, 1, 1)
 NT = (((1,), (1,)), ((), ()))
 
@@ -46,34 +47,65 @@
     return tables.astype(np.float32).astype(jnp.bfloat16)
 
 
-def filter_kernel(
-    volt_hbm, margin, window_hbm, waves_hbm, order_hbm, slots_hbm, out,
-    volt, window, slots, waves, order, blocks, spectra, sorted_, pick, rows, sems,
+def tap_sums(window, volt_of, blocks, frames, first, last):
+    inputs = blocks.shape[1] // frames
+
+    def chunk(j, carry):
+        low = pl.multiple_of(j * 128, 128)
+        sums = []
+        for at in (low, pl.multiple_of(low + HALF, 128)):
+            weights = [
+                jnp.broadcast_to(window[:, pl.ds(t * DFT + at, 128)], (inputs, 128))
+                for t in range(TAPS)
+            ]
+            held = [volt_of(first + t + 1 - TAPS, at) for t in range(TAPS - 1)]
+            column = []
+            for f in range(first, last):
+                held.append(volt_of(f, at))
+                total = None
+                for t in range(TAPS):
+                    if held[t] is not None:
+                        term = held[t] * weights[t]
+                        total = term if total is None else total + term
+                held = held[1:]
+                column.append(total)
+            sums.append(column)
+        for f in range(0, last - first, 2):
+            for parity in range(2):
+                pair = []
+                for k in (f, f + 1):
+                    low_sum, high_sum = sums[0][k], sums[1][k]
+                    pair.append(low_sum - high_sum if parity else low_sum + high_sum)
+                at = (first + f) * inputs
+                blocks[parity, at : at + 2 * inputs, pl.ds(low, 128)] = jnp.concatenate(
+                    pair, axis=0
+                ).astype(jnp.bfloat16)
+        return carry
+
+    lax.fori_loop(0, HALF // 128, chunk, 0)
+
+
+def sums_kernel(
+    chans, volt_hbm, window_hbm, slots_hbm, waves_hbm, order_hbm,
+    blocks, pick, head, window, waves, order, volt, slots, sems,
 ):
     inputs = volt.shape[0]
     frames = volt.shape[1] // DFT
-    dests = out.shape[0] // inputs
-    chans = slots.shape[1] // dests
-    scale = 1.0 / math.sqrt(TAPS * CHANNELS)
+    dests = pick.shape[0] // chans
     group = frames // GROUPS
     span = group * DFT
     copies = [
-        pltpu.make_async_copy(
-            volt_hbm.at[:, pl.ds(g * span, span)], volt.at[:, pl.ds(g * span, span)], sems.at[g]
-        )
-        for g in range(GROUPS)
+        pltpu.make_async_copy(slots_hbm, slots, sems.at[GROUPS]),
+        pltpu.make_async_copy(window_hbm, window, sems.at[GROUPS + 1]),
     ]
-    for parity in range(2):
+    for g in range(GROUPS):
         copies.append(
             pltpu.make_async_copy(
-                waves_hbm.at[parity], waves.at[parity], sems.at[GROUPS + parity]
+                volt_hbm.at[:, pl.ds(g * span, span)], volt.at[:, pl.ds(g * span, span)], sems.at[g]
             )
         )
-    copies.append(pltpu.make_async_copy(order_hbm, order, sems.at[GROUPS + 2]))
-    taps_copy = pltpu.make_async_copy(window_hbm, window, sems.at[GROUPS + 3])
-    taps_copy.start()
-    slots_copy = pltpu.make_async_copy(slots_hbm, slots, sems.at[GROUPS + 4])
-    slots_copy.start()
+    copies.append(pltpu.make_async_copy(waves_hbm, waves, sems.at[GROUPS + 2]))
+    copies.append(pltpu.make_async_copy(order_hbm, order, sems.at[GROUPS + 3]))
     for copy in copies:
         copy.start()
 
@@ -81,7 +113,7 @@
     place = lax.broadcasted_iota(jnp.int32, (dests, CHANNELS), 1)
     channel = jnp.where(place < half_ch, 2 * place, 2 * (place - half_ch) + 1)
     dest = lax.broadcasted_iota(jnp.int32, (dests, CHANNELS), 0)
-    slots_copy.wait()
+    copies[0].wait()
     held_by = slots[...].astype(jnp.float32)
     for c in range(chans):
         wanted = jnp.sum(
@@ -90,59 +122,40 @@
         pick[c * dests : (c + 1) * dests, :] = (
             (channel == wanted).astype(jnp.float32).astype(jnp.bfloat16)
         )
-    taps_copy.wait()
-
-    def fold(g):
-        def chunk(j, carry):
-            low = pl.multiple_of(j * 128, 128)
-            sums = []
-            for at in (low, pl.multiple_of(low + HALF, 128)):
-                weights = [
-                    jnp.broadcast_to(window[:, pl.ds(t * DFT + at, 128)] * scale, (inputs, 128))
-                    for t in range(TAPS)
-                ]
-
-                def frame(f):
-                    if f < 0:
-                        value = margin[:, pl.ds((f + TAPS - 1) * DFT + at, 128)]
-                    else:
-                        value = volt[:, pl.ds(f * DFT + at, 128)]
-                    return value.astype(jnp.float32)
-
-                held = [frame(g * group + t + 1 - TAPS) for t in range(TAPS - 1)]
-                column = []
-                for f in range(g * group, (g + 1) * group):
-                    held.append(frame(f))
-                    total = held[0] * weights[0]
-                    for t in range(1, TAPS):
-                        total = total + held[t] * weights[t]
-                    held = held[1:]
-                    column.append(total)
-                sums.append(column)
-            for f in range(0, group, 2):
-                for parity in range(2):
-                    pair = []
-                    for k in (f, f + 1):
-                        first, second = sums[0][k], sums[1][k]
-                        pair.append(first - second if parity else first + second)
-                    at = (g * group + f) * inputs
-                    blocks[parity, at : at + 2 * inputs, pl.ds(low, 128)] = jnp.concatenate(
-                        pair, axis=0
-                    ).astype(jnp.bfloat16)
-            return carry
-
-        lax.fori_loop(0, HALF // 128, chunk, 0)
+    copies[1].wait()
+    window[...] = window[...] * (1.0 / math.sqrt(TAPS * CHANNELS))
+
+    def volt_of(f, at):
+        return None if f < 0 else volt[:, pl.ds(f * DFT + at, 128)].astype(jnp.float32)
 
     for g in range(GROUPS):
-        copies[g].wait()
-        fold(g)
-
+        copies[2 + g].wait()
+        tap_sums(window, volt_of, blocks, frames, g * group, (g + 1) * group)
+    head[...] = volt[:, : head.shape[1]]
+    for copy in copies[2 + GROUPS :]:
+        copy.wait()
+
+
+def spectra_kernel(
+    blocks, margin, head, window, pick, waves, order, out, first, spectra, sorted_, rows
+):
+    inputs = head.shape[0]
+    columns = blocks.shape[1]
+    frames = columns // inputs
+    dests = out.shape[0] // inputs
+    chans = pick.shape[0] // dests
+    half_ch = CHANNELS // 2
+
+    def volt_of(f, at):
+        source, f = (margin, f + TAPS - 1) if f < 0 else (head, f)
+        return source[:, pl.ds(f * DFT + at, 128)].astype(jnp.float32)
+
+    tap_sums(window, volt_of, first, HEAD, 0, HEAD)
     for parity in range(2):
-        copies[GROUPS + parity].wait()
+        sums = jnp.concatenate([first[parity], blocks[parity, HEAD * inputs :, :]], axis=0)
         spectra[:, parity * CHANNELS : (parity + 1) * CHANNELS] = jnp.dot(
-            blocks[parity], waves[parity], preferred_element_type=jnp.float32
+            sums, waves[parity], preferred_element_type=jnp.float32
         ).astype(jnp.bfloat16)
-    copies[GROUPS + 2].wait()
     for parity in range(2):
         for part in range(2):
             at = parity * CHANNELS + part * half_ch
@@ -177,42 +190,61 @@
             ).astype(jnp.bfloat16)
 
 
+def tap_blocks(volt, window, slots, dests):
+    inputs, own = volt.shape
+    chans = slots.shape[1] // dests
+    vmem = pl.BlockSpec(memory_space=pltpu.VMEM)
+    hbm = pl.BlockSpec(memory_space=pltpu.HBM)
+    waves, order = jnp.asarray(wave_columns()), jnp.asarray(order_table(inputs, own // DFT))
+    return pl.pallas_call(
+        lambda *refs: sums_kernel(chans, *refs),
+        in_specs=[hbm] * 5,
+        out_specs=[vmem] * 6,
+        out_shape=[
+            jax.ShapeDtypeStruct((2, inputs * own // DFT, HALF), jnp.bfloat16),
+            jax.ShapeDtypeStruct((chans * dests, CHANNELS), jnp.bfloat16),
+            jax.ShapeDtypeStruct((inputs, HEAD * DFT), jnp.bfloat16),
+            jax.ShapeDtypeStruct(window.shape, jnp.float32),
+            jax.ShapeDtypeStruct(waves.shape, jnp.bfloat16),
+            jax.ShapeDtypeStruct(order.shape, jnp.bfloat16),
+        ],
+        scratch_shapes=[
+            pltpu.VMEM(volt.shape, jnp.bfloat16),
+            pltpu.VMEM(slots.shape, jnp.int32),
+            pltpu.SemaphoreType.DMA((GROUPS + 4,)),
+        ],
+        compiler_params=pltpu.CompilerParams(vmem_limit_bytes=VMEM),
+        cost_estimate=pl.CostEstimate(
+            flops=2 * inputs * own * TAPS, bytes_accessed=8 << 20, transcendentals=0
+        ),
+        name="tap_sums",
+    )(*(pltpu.with_memory_space_constraint(x, pltpu.HBM) for x in (volt, window, slots, waves, order)))
+
+
 def filtered(volt, margin, window, slots, dests):
     inputs, own = volt.shape
     frames = own // DFT
     chans = slots.shape[1] // dests
     columns = inputs * frames
     vmem = pl.BlockSpec(memory_space=pltpu.VMEM)
-    hbm = pl.BlockSpec(memory_space=pltpu.HBM)
-    waves, order = jnp.asarray(wave_columns()), jnp.asarray(order_table(inputs, frames))
-    volt, window, waves, order, slots = (
-        pltpu.with_memory_space_constraint(array, pltpu.HBM)
-        for array in (volt, window, waves, order, slots)
-    )
+    blocks, pick, head, taps, waves, order = tap_blocks(volt, window, slots, dests)
     return pl.pallas_call(
-        filter_kernel,
-        in_specs=[hbm, vmem, hbm, hbm, hbm, hbm],
+        spectra_kernel,
+        in_specs=[vmem] * 7,
         out_specs=vmem,
         out_shape=jax.ShapeDtypeStruct((dests * inputs, chans * 2 * frames), jnp.bfloat16),
         scratch_shapes=[
-            pltpu.VMEM(volt.shape, jnp.bfloat16),
-            pltpu.VMEM(window.shape, jnp.float32),
-            pltpu.VMEM(slots.shape, jnp.int32),
-            pltpu.VMEM(waves.shape, jnp.bfloat16),
-            pltpu.VMEM(order.shape, jnp.bfloat16),
-            pltpu.VMEM((2, columns, HALF), jnp.bfloat16),
+            pltpu.VMEM((2, HEAD * inputs, HALF), jnp.bfloat16),
             pltpu.VMEM((columns, 2 * CHANNELS), jnp.bfloat16),
             pltpu.VMEM((2 * columns, CHANNELS), jnp.bfloat16),
-            pltpu.VMEM((chans * dests, CHANNELS), jnp.bfloat16),
             pltpu.VMEM((chans * dests * (inputs + 1), 2 * frames), jnp.float32),
-            pltpu.SemaphoreType.DMA((GROUPS + 5,)),
         ],
         compiler_params=pltpu.CompilerParams(vmem_limit_bytes=VMEM),
         cost_estimate=pl.CostEstimate(
             flops=2 * columns * CHANNELS * 4 * 1024, bytes_accessed=8 << 20, transcendentals=0
         ),
-        name="polyphase",
-    )(volt, margin, window, waves, order, slots)
+        name="spectra",
+    )(blocks, margin, head, taps, pick, waves, order)
 
 
 def beam_kernel(scale, own, layout, tables, out, mixer, mixed):

time: 87.3 us -> 84.2 us (0.964)
  waiting for transfers between devices: 10.7 us -> 9.05 us
  starting transfers between devices: 13.2 us -> 12.3 us
    ppermute x1, waiting for transfers between devices: 1.62 us -> 0.01 us  [on_device(): lax.ppermute(voltages[:, own_samples - (TAPS - 1) * DFT:], 'rep', [(0, 1)])]
    pallas_call x1 -> x2, Pallas kernels: 5.87 us -> 5.7 us  [the longest x1 3.03 us: tap_blocks(): pl.pallas_call(lambda *refs: sums_kernel(chans, *refs), in_specs=[hbm] *...]
  transfers between devices with their start and end apart: 5 -> 5, of which waited for: 4 -> 3; matrix products, arithmetic and copies ran while one was open for 0% -> 0% of each run, Pallas kernels for 12% -> 16%
where the time goes in v3:
time: 84.2 us; the launch traced here: 83.4 us
  blocking collectives  42.1 us (50%)
  Pallas kernels  18.2 us (22%)
  starting transfers between devices  12.3 us (15%)
  waiting for transfers between devices  9.05 us (11%)
  local copies, waits for them, and re-layouts  1.02 us (1%)
    all_to_all x1, blocking collectives, on_device(): lax.all_to_all(outgoing, 'feed', split_axis=0, concat_axis=0, tiled=True)  42.1 us
    pallas_call x3, Pallas kernels, gram(): pl.pallas_call(lambda *refs: gram_kernel(1.0 / total_frames, *refs), grid...  8.39 us
    ppermute x3, starting transfers between devices, on_device(): lax.ppermute(source[:, at * 128:(at + part) * 128], 'rep', swap)  6.59 us
    ppermute x1, starting transfers between devices, on_device(): lax.ppermute(voltages[:, own_samples - (TAPS - 1) * DFT:], 'rep', [(0, 1)])  5.64 us
    ppermute x3, waiting for transfers between devices, on_device(): lax.ppermute(source[:, at * 128:(at + part) * 128], 'rep', swap)  5.32 us
    pallas_call x1, Pallas kernels, beams(): pl.pallas_call(lambda *refs: beam_kernel(scale, *refs), out_shape=jax.Sha...  4.14 us
    ppermute x1, waiting for transfers between devices, on_device(): beam_other = lax.ppermute(beam_own, 'rep', swap)  3.73 us
    pallas_call x1, Pallas kernels, tap_blocks(): pl.pallas_call(lambda *refs: sums_kernel(chans, *refs), in_specs=[hbm] *...  3.03 us
  transfers between devices with their start and end apart: 5, of which 3 were waited for; matrix products, arithmetic and copies ran while one was open for 0% of the time, Pallas kernels for 16%

profile of v3, /device:TPU:1, one launch (start us, length us, event | category | flops | bytes accessed | tf_op | source)
XLA Modules:
  0.0 83.4 jit_solution(7202361646845173574)
XLA Ops:
  0.6 0.9 %slice.12 = bf16[8,6144]{1,0:T(8,128)(2,1)S(1)} slice(bf16[8,131072]{1,0:T(8,128)(2,1)} %refs_0_.1), slice={[0:8], [124928:131072]} | slice | bytes 196608 | tf_op jit(solution)/shard_map/slice | solution.py:384
  1.5 5.6 %collective-permute-start = (bf16[8,6144]{1,0:T(8,128)(2,1)S(1)}, bf16[8,6144]{1,0:T(8,128)(2,1)S(1)}, u32[]{:S(2)}, u32[]{:S(2)}) collective-permute-start(bf16[8,6144]{1,0:T(8,128)(2,1)S(1)} %slice.12), channel_id=1, source_target_pairs={{0,1},{2,3},{4,5},{6,7},{8,9},{10,11},{12,13},{14,15},{16,17},{18,... | collective-permute-start | bytes 294920 | tf_op jit(solution)/shard_map/ppermute | solution.py:384
  7.2 3.0 %tap_sums.1 = (bf16[2,512,1024]{2,1,0:T(8,128)(2,1)S(1)}, bf16[512,512]{1,0:T(8,128)(2,1)S(1)}, bf16[8,8192]{1,0:T(8,128)(2,1)S(1)}, f32[1,8192]{1,0:T(1,128)S(1...) custom-call(bf16[8,131072]{1,0:T(8,128)(2,1)} %refs_0_.1, f32[1,8192]{1,0:T(1,128)} %bitcast.21, ...), custom_call_target="tpu_custom_call" | custom-call | flops 8388608 | bytes 8388608 | tf_op jit(solution)/shard_map/tap_sums/pallas_call | solution.py:199
  10.2 0.0 collective-permute-done.margin
  10.2 2.7 %spectra.1 = bf16[1024,512]{1,0:T(8,128)(2,1)S(1)} custom-call(bf16[2,512,1024]{2,1,0:T(8,128)(2,1)S(1)} %get-tuple-element.11.blocks, bf16[8,6144]{1,0:T(8,128)(2,1)S(1)} %collective-permute-done.margin, bf16[8,8192]{1,0:T(8,128)(2,1)S(1)} %get-tuple-element.12.head, f32[1,8192]{1,0:T(1,128)S(1)} %get-tuple-element.13.window, ...), custom_call_target="tpu_custom_call" | custom-call | flops 2147483648 | bytes 8388608 | tf_op jit(solution)/shard_map/spectra/pallas_call | solution.py:231
  12.9 0.0 copy-start
  12.9 0.0 copy-start.1
  12.9 42.1 %all_to_all.11 = bf16[128,8,512]{2,1,0:T(8,128)(2,1)S(1)} all-to-all(bf16[128,8,512]{2,1,0:T(8,128)(2,1)S(1)} %bitcast.18), channel_id=1, replica_groups=mesh['feed'=128,'rep'=2] {'feed'}, dimensions={0} | all-to-all | bytes 2097152 | tf_op jit(solution)/shard_map/all_to_all | solution.py:388
  55.0 3.5 %collective-permute-start.3 = (bf16[1024,256]{1,0:T(8,128)(2,1)S(1)}, bf16[1024,256]{1,0:T(8,128)(2,1)S(1)}, u32[]{:S(2)}, u32[]{:S(2)}) collective-permute-start(bf16[1024,256]{1,0:T(8,128)(2,1)S(1)} %slice.17), channel_id=1, source_target_pairs={{0,1},{1,0},{2,3},{3,2},{4,5},{5,4},{6,7},{7,6},{8,9},{9,8},{10,11... | collective-permute-start | bytes 1572872 | tf_op jit(solution)/shard_map/ppermute | solution.py:393
  58.5 0.1 collective-permute-start.2
  58.6 0.0 copy-done
  58.6 0.0 copy-done.1
  58.6 4.1 %beams.1.refs_4_ = f32[8,512]{1,0:T(8,128)S(1)} custom-call(bf16[1024,512]{1,0:T(8,128)(2,1)S(1)} %bitcast.13, s32[1,1024]{1,0:T(1,128)S(1)} %bitcast.19, bf16[256,128]{1,0:T(8,128)(2,1)S(1)} %copy-done.1), custom_call_target="tpu_custom_call" | custom-call | flops 2147483648 | bytes 4194304 | tf_op jit(solution)/shard_map/beams/pallas_call | solution.py:293
  62.8 3.0 %collective-permute-start.1 = (bf16[1024,128]{1,0:T(8,128)(2,1)S(1)}, bf16[1024,128]{1,0:T(8,128)(2,1)S(1)}, u32[]{:S(2)}, u32[]{:S(2)}) collective-permute-start(bf16[1024,128]{1,0:T(8,128)(2,1)S(1)} %slice.13), channel_id=1, source_target_pairs={{0,1},{1,0},{2,3},{3,2},{4,5},{5,4},{6,7},{7,6},{8,9},{9,8},{10,11... | collective-permute-start | bytes 786440 | tf_op jit(solution)/shard_map/ppermute | solution.py:393
  65.9 0.1 collective-permute-start.4
  66.0 3.6 %collective-permute-done.3.refs_2_ = bf16[1024,256]{1,0:T(8,128)(2,1)S(1)} collective-permute-done((bf16[1024,256]{1,0:T(8,128)(2,1)S(1)}, bf16[1024,256]{1,0:T(8,128)(2,1)S(1)}, u32[]{:S(2)}, u32[]{:S(2)}) %collective-permute-start.3) | collective-permute-done | bytes 524320 | tf_op jit(solution)/shard_map/ppermute | solution.py:393
  69.6 3.9 %gram.3.refs_3_ = bf16[256,8,16,128]{3,2,1,0:T(8,128)(2,1)} custom-call(s32[1]{0:T(128)} %bitcast.refs_0_, bf16[1024,512]{1,0:T(8,128)(2,1)S(1)} %bitcast.15, bf16[1024,256]{1,0:T(8,128)(2,1)S(1)} %collective-permute-done.3.refs_2_), custom_call_target="tpu_custom_call" | custom-call | flops 1073741824 | bytes 4194304 | tf_op jit(solution)/shard_map/gram/pallas_call | solution.py:360
  73.5 1.7 %collective-permute-done.2.refs_2_ = bf16[1024,128]{1,0:T(8,128)(2,1)S(1)} collective-permute-done((bf16[1024,128]{1,0:T(8,128)(2,1)S(1)}, bf16[1024,128]{1,0:T(8,128)(2,1)S(1)}, u32[]{:S(2)}, u32[]{:S(2)}) %collective-permute-start.2) | collective-permute-done | bytes 262176 | tf_op jit(solution)/shard_map/ppermute | solution.py:393
  75.2 2.2 %gram.4.refs_3_ = bf16[256,8,16,128]{3,2,1,0:T(8,128)(2,1)} custom-call(s32[1]{0:T(128)} %bitcast.refs_0_, bf16[1024,512]{1,0:T(8,128)(2,1)S(1)} %bitcast.16, bf16[1024,128]{1,0:T(8,128)(2,1)S(1)} %collective-permute-done.2.refs_2_, bf16[256,8,16,128]{3,2,1,0:T(8,128)(2,1)} %gram.3.refs_3_), custom_call_target="tpu_custom_call", output_to_operand_aliasing={{}: (3, {})} | custom-call | flops 536870912 | bytes 2097152 | tf_op jit(solution)/shard_map/gram/pallas_call | solution.py:360
  77.4 3.7 %collective-permute-done.4.refs_5_ = f32[8,512]{1,0:T(8,128)S(1)} collective-permute-done((f32[8,512]{1,0:T(8,128)S(1)}, f32[8,512]{1,0:T(8,128)S(1)}, u32[]{:S(2)}, u32[]{:S(2)}) %collective-permute-start.4) | collective-permute-done | bytes 16416 | tf_op jit(solution)/shard_map/ppermute | solution.py:395
  81.1 0.0 collective-permute-done.1.refs_2_
  81.1 2.3 %gram.5 = (bf16[256,8,16,128]{3,2,1,0:T(8,128)(2,1)}, f32[8,512]{1,0:T(8,128)}) custom-call(s32[1]{0:T(128)} %bitcast.refs_0_, bf16[1024,512]{1,0:T(8,128)(2,1)S(1)} %bitcast.17, bf16[1024,128]{1,0:T(8,128)(2,1)S(1)} %collective-permute-done.1.refs_2_, bf16[256,8,16,128]{3,2,1,0:T(8,128)(2,1)} %gram.4.refs_3_, ...), custom_call_target="tpu_custom_call", output_to_operand_aliasing={{0}: (3, {})} | custom-call | flops 536870912 | bytes 2097152 | tf_op jit(solution)/shard_map/gram/pallas_call | solution.py:360
  (3 shorter events, 0.1 us)
Async XLA Ops:
  1.5 8.7 %collective-permute-start = (bf16[8,6144]{1,0:T(8,128)(2,1)S(1)}, bf16[8,6144]{1,0:T(8,128)(2,1)S(1)}, u32[]{:S(2)}, u32[]{:S(2)}) collective-permute-start(bf16[8,6144]{1,0:T(8,128)(2,1)S(1)} %slice.12), channel_id=1, source_target_pairs={{0,1},{2,3},{4,5},{6,7},{8,9},{10,11},{12,13},{14,15},{16,17},{18,... | collective-permute-start | bytes 294920 | tf_op jit(solution)/shard_map/ppermute | solution.py:384
  12.9 45.7 %copy-start = (s32[1024]{0:T(1024)S(1)}, s32[1024]{0:T(1024)}, u32[]{:S(2)}) copy-start(s32[1024]{0:T(1024)} %param.10) | copy-start | bytes 12292
  12.9 45.7 %copy-start.1 = (bf16[256,128]{1,0:T(8,128)(2,1)S(1)}, bf16[256,128]{1,0:T(8,128)(2,1)}, u32[]{:S(2)}) copy-start(bf16[256,128]{1,0:T(8,128)(2,1)} %constant.12.clone.refs_2_) | copy-start | bytes 196612
  55.0 14.5 %collective-permute-start.3 = (bf16[1024,256]{1,0:T(8,128)(2,1)S(1)}, bf16[1024,256]{1,0:T(8,128)(2,1)S(1)}, u32[]{:S(2)}, u32[]{:S(2)}) collective-permute-start(bf16[1024,256]{1,0:T(8,128)(2,1)S(1)} %slice.17), channel_id=1, source_target_pairs={{0,1},{1,0},{2,3},{3,2},{4,5},{5,4},{6,7},{7,6},{8,9},{9,8},{10,11... | collective-permute-start | bytes 1572872 | tf_op jit(solution)/shard_map/ppermute | solution.py:393
  58.5 16.7 %collective-permute-start.2 = (bf16[1024,128]{1,0:T(8,128)(2,1)S(1)}, bf16[1024,128]{1,0:T(8,128)(2,1)S(1)}, u32[]{:S(2)}, u32[]{:S(2)}) collective-permute-start(bf16[1024,128]{1,0:T(8,128)(2,1)S(1)} %slice.16), channel_id=1, source_target_pairs={{0,1},{1,0},{2,3},{3,2},{4,5},{5,4},{6,7},{7,6},{8,9},{9,8},{10,11... | collective-permute-start | bytes 786440 | tf_op jit(solution)/shard_map/ppermute | solution.py:393
  62.8 18.3 %collective-permute-start.1 = (bf16[1024,128]{1,0:T(8,128)(2,1)S(1)}, bf16[1024,128]{1,0:T(8,128)(2,1)S(1)}, u32[]{:S(2)}, u32[]{:S(2)}) collective-permute-start(bf16[1024,128]{1,0:T(8,128)(2,1)S(1)} %slice.13), channel_id=1, source_target_pairs={{0,1},{1,0},{2,3},{3,2},{4,5},{5,4},{6,7},{7,6},{8,9},{9,8},{10,11... | collective-permute-start | bytes 786440 | tf_op jit(solution)/shard_map/ppermute | solution.py:393
  65.9 15.3 %collective-permute-start.4 = (f32[8,512]{1,0:T(8,128)S(1)}, f32[8,512]{1,0:T(8,128)S(1)}, u32[]{:S(2)}, u32[]{:S(2)}) collective-permute-start(f32[8,512]{1,0:T(8,128)S(1)} %beams.1.refs_4_), channel_id=1, source_target_pairs={{0,1},{1,0},{2,3},{3,2},{4,5},{5,4},{6,7},{7,6},{8,9},{9,8},{10,11... | collective-permute-start | bytes 49160 | tf_op jit(solution)/shard_map/ppermute | solution.py:395

commit v4 on v3

--- a/solution.py
+++ b/solution.py
@@ -17,6 +17,7 @@
 HALF = DFT // 2
 VMEM = 24 * 1024 * 1024
 GROUPS = 4
+PIECE = 64
 HEAD = 4
 PARTS = (2, 1, 1)
 NT = (((1,), (1,)), ((), ()))
@@ -30,14 +31,6 @@
         angles = (samples[:, None] * bins[None, :] % DFT) * (2.0 * np.pi / DFT)
         tables.append(np.concatenate([np.cos(angles), -np.sin(angles)], axis=1))
     return np.stack(tables).astype(np.float32).astype(jnp.bfloat16)
-
-
-def order_table(inputs, frames):
-    frame, feed = np.meshgrid(np.arange(frames), np.arange(inputs), indexing="ij")
-    target = (feed * frames + frame).reshape(-1)
-    table = np.zeros((target.size, target.size), np.float32)
-    table[target, np.arange(target.size)] = 1.0
-    return table.astype(jnp.bfloat16)
 
 
 def position_tables():
@@ -86,7 +79,7 @@
 
 
 def sums_kernel(
-    chans, volt_hbm, window_hbm, slots_hbm, waves_hbm, order_hbm,
+    chans, volt_hbm, window_hbm, slots_hbm, waves_hbm,
     blocks, pick, head, window, waves, order, volt, slots, sems,
 ):
     inputs = volt.shape[0]
@@ -105,7 +98,6 @@
             )
         )
     copies.append(pltpu.make_async_copy(waves_hbm, waves, sems.at[GROUPS + 2]))
-    copies.append(pltpu.make_async_copy(order_hbm, order, sems.at[GROUPS + 3]))
     for copy in copies:
         copy.start()
 
@@ -122,6 +114,10 @@
         pick[c * dests : (c + 1) * dests, :] = (
             (channel == wanted).astype(jnp.float32).astype(jnp.bfloat16)
         )
+    row = lax.broadcasted_iota(jnp.int32, order.shape, 0)
+    column = lax.broadcasted_iota(jnp.int32, order.shape, 1)
+    source = (row % frames) * inputs + row // frames
+    order[...] = (column == source).astype(jnp.float32).astype(jnp.bfloat16)
     copies[1].wait()
     window[...] = window[...] * (1.0 / math.sqrt(TAPS * CHANNELS))
 
@@ -195,10 +191,10 @@
     chans = slots.shape[1] // dests
     vmem = pl.BlockSpec(memory_space=pltpu.VMEM)
     hbm = pl.BlockSpec(memory_space=pltpu.HBM)
-    waves, order = jnp.asarray(wave_columns()), jnp.asarray(order_table(inputs, own // DFT))
+    waves = jnp.asarray(wave_columns())
     return pl.pallas_call(
         lambda *refs: sums_kernel(chans, *refs),
-        in_specs=[hbm] * 5,
+        in_specs=[hbm] * 4,
         out_specs=[vmem] * 6,
         out_shape=[
             jax.ShapeDtypeStruct((2, inputs * own // DFT, HALF), jnp.bfloat16),
@@ -206,19 +202,19 @@
             jax.ShapeDtypeStruct((inputs, HEAD * DFT), jnp.bfloat16),
             jax.ShapeDtypeStruct(window.shape, jnp.float32),
             jax.ShapeDtypeStruct(waves.shape, jnp.bfloat16),
-            jax.ShapeDtypeStruct(order.shape, jnp.bfloat16),
+            jax.ShapeDtypeStruct((inputs * own // DFT,) * 2, jnp.bfloat16),
         ],
         scratch_shapes=[
             pltpu.VMEM(volt.shape, jnp.bfloat16),
             pltpu.VMEM(slots.shape, jnp.int32),
-            pltpu.SemaphoreType.DMA((GROUPS + 4,)),
+            pltpu.SemaphoreType.DMA((GROUPS + 3,)),
         ],
         compiler_params=pltpu.CompilerParams(vmem_limit_bytes=VMEM),
         cost_estimate=pl.CostEstimate(
             flops=2 * inputs * own * TAPS, bytes_accessed=8 << 20, transcendentals=0
         ),
         name="tap_sums",
-    )(*(pltpu.with_memory_space_constraint(x, pltpu.HBM) for x in (volt, window, slots, waves, order)))
+    )(*(pltpu.with_memory_space_constraint(x, pltpu.HBM) for x in (volt, window, slots, waves)))
 
 
 def filtered(volt, margin, window, slots, dests):
@@ -237,7 +233,7 @@
             pltpu.VMEM((2, HEAD * inputs, HALF), jnp.bfloat16),
             pltpu.VMEM((columns, 2 * CHANNELS), jnp.bfloat16),
             pltpu.VMEM((2 * columns, CHANNELS), jnp.bfloat16),
-            pltpu.VMEM((chans * dests * (inputs + 1), 2 * frames), jnp.float32),
+            pltpu.VMEM(((chans * dests + 8) * (inputs + 1), 2 * frames), jnp.float32),
         ],
         compiler_params=pltpu.CompilerParams(vmem_limit_bytes=VMEM),
         cost_estimate=pl.CostEstimate(
@@ -305,36 +301,58 @@
     )(own, layout, position_tables())
 
 
-def gram_kernel(scale, rep, own, other, *refs):
-    out, rows = refs[-2:]
-    if len(refs) > 3:
-        beam_own, beam_other, out, beam, rows = refs[-5:]
+def gram_kernel(scale, first, rep, own, other, *refs):
+    out, rows, stage, sems = refs[-4:]
+    copies = []
+    if len(refs) > 5:
+        beam_own, beam_other, out, beam_out, beam, rows, stage, sems = refs[-8:]
         beam[...] = beam_own[...] + beam_other[...]
-    step = pl.program_id(0)
+        copies.append(pltpu.make_async_copy(beam, beam_out, sems.at[0]))
+        copies[0].start()
     count, _, tiles, _ = out.shape
     inputs = own.shape[0]
     pitch = tiles + 1
-    start = pl.multiple_of((step % 2) * (inputs // 2) + rep[0] * count, count)
     lane = lax.broadcasted_iota(jnp.int32, (count, 128), 1)
-    plain, turned = [], []
-    for source in (own, other):
-        part = source[pl.ds(start, count), :]
-        plain.append(part)
-        swapped = pltpu.roll(part.astype(jnp.float32), 64, 1)
-        turned.append(jnp.where(lane < 64, swapped, -swapped).astype(jnp.bfloat16))
-    left = jnp.concatenate(
-        [jnp.concatenate(plain, axis=1), jnp.concatenate(turned, axis=1)], axis=0
-    )
-    for at in range(0, inputs, 256):
-        right = jnp.concatenate([own[at : at + 256, :], other[at : at + 256, :]], axis=1)
-        products = lax.dot_general(left, right, NT, preferred_element_type=jnp.float32)
-        for tile in range(2):
-            for part in range(2):
-                rows[pl.ds((at // 128 + tile) * 2 + part, count, stride=pitch), :] = products[
-                    part * count : (part + 1) * count, tile * 128 : (tile + 1) * 128
-                ]
-    for r in range(count):
-        out[r, 0] = (rows[r * pitch : r * pitch + tiles, :] * scale).astype(jnp.bfloat16)
+    for c in range(other.shape[1] // 128):
+        mine = pl.ds((first + c) * 128, 128)
+        theirs = pl.ds(c * 128, 128)
+        left = []
+        for half in range(2):
+            start = pl.multiple_of(half * (inputs // 2) + rep[0] * count, count)
+            plain, turned = [], []
+            for part in (own[pl.ds(start, count), mine], other[pl.ds(start, count), theirs]):
+                plain.append(part)
+                swapped = pltpu.roll(part.astype(jnp.float32), 64, 1)
+                turned.append(jnp.where(lane < 64, swapped, -swapped).astype(jnp.bfloat16))
+            left += [jnp.concatenate(plain, axis=1), jnp.concatenate(turned, axis=1)]
+        left = jnp.concatenate(left, axis=0)
+        for at in range(0, inputs, 256):
+            right = jnp.concatenate([own[at : at + 256, mine], other[at : at + 256, theirs]], axis=1)
+            products = lax.dot_general(left, right, NT, preferred_element_type=jnp.float32)
+            for half in range(2):
+                for part in range(2):
+                    for tile in range(2):
+                        to = half * count * pitch + (at // 128 + tile) * 2 + part
+                        row = (2 * half + part) * count
+                        rows[pl.ds(to, count, stride=pitch), :] = products[
+                            row : row + count, tile * 128 : (tile + 1) * 128
+                        ]
+        for half in range(2):
+            slot = 2 * c + half
+            for piece in range(0, count, PIECE):
+                for r in range(piece, piece + PIECE):
+                    at = (half * count + r) * pitch
+                    stage[slot, r] = (rows[at : at + tiles, :] * scale).astype(jnp.bfloat16)
+                copies.append(
+                    pltpu.make_async_copy(
+                        stage.at[slot, pl.ds(piece, PIECE)],
+                        out.at[pl.ds(piece, PIECE), 2 * first + slot],
+                        sems.at[len(copies)],
+                    )
+                )
+                copies[-1].start()
+    for copy in copies:
+        copy.wait()
 
 
 def gram(rep, own, other, first, extra, count, total_frames):
@@ -342,35 +360,37 @@
     slots = 2 * (wide // 128)
     steps = 2 * (other.shape[1] // 128)
     tiles = inputs // 64
-    ops = [rep, own, other, *extra]
-    specs = [
-        pl.BlockSpec(memory_space=pltpu.SMEM),
-        pl.BlockSpec((inputs, 128), lambda s: (0, first + s // 2)),
-        pl.BlockSpec((inputs, 128), lambda s: (0, s // 2)),
-    ]
-    out_specs = [pl.BlockSpec((count, 1, tiles, 128), lambda s: (0, s + 2 * first, 0, 0))]
+    vmem = pl.BlockSpec(memory_space=pltpu.VMEM)
+    hbm = pl.BlockSpec(memory_space=pltpu.HBM)
+    specs = [pl.BlockSpec(memory_space=pltpu.SMEM), vmem, vmem]
+    out_specs = [hbm]
     out_shape = [jax.ShapeDtypeStruct((count, slots, tiles, 128), jnp.bfloat16)]
+    scratch = []
     if extra:
-        specs.append(pl.BlockSpec(memory_space=pl.ANY))
+        specs.append(hbm)
     if len(extra) > 1:
-        small = pl.BlockSpec(extra[1].shape, lambda s: (0, 0))
-        specs += [small, small]
-        out_specs.append(small)
+        specs += [vmem, vmem]
+        out_specs.append(hbm)
         out_shape.append(jax.ShapeDtypeStruct(extra[1].shape, jnp.float32))
+        scratch.append(pltpu.VMEM(extra[1].shape, jnp.float32))
     return pl.pallas_call(
-        lambda *refs: gram_kernel(1.0 / total_frames, *refs),
-        grid=(steps,),
+        lambda *refs: gram_kernel(1.0 / total_frames, first, *refs),
         in_specs=specs,
         out_specs=out_specs,
         out_shape=out_shape,
-        scratch_shapes=[pltpu.VMEM((count * (tiles + 1), 128), jnp.float32)],
+        scratch_shapes=scratch
+        + [
+            pltpu.VMEM(((2 * count + 8) * (tiles + 1), 128), jnp.float32),
+            pltpu.VMEM((steps, count, tiles, 128), jnp.bfloat16),
+            pltpu.SemaphoreType.DMA((1 + steps * (count // PIECE),)),
+        ],
         input_output_aliases={3: 0} if extra else {},
         compiler_params=pltpu.CompilerParams(vmem_limit_bytes=VMEM),
         cost_estimate=pl.CostEstimate(
             flops=4 * steps * count * inputs * 256, bytes_accessed=steps << 20, transcendentals=0
         ),
         name="gram",
-    )(*ops)
+    )(rep, own, other, *extra)
 
 
 def on_device(voltages, pfb_window, channel_map, beam_layout):

time: 84.2 us -> 84.1 us (level)
  Pallas kernels: 18.2 us -> 16.8 us
  waiting for transfers between devices: 9.05 us -> 10.1 us
    pallas_call x3, Pallas kernels: 8.39 us -> 6.88 us  [gram(): pl.pallas_call(lambda *refs: gram_kernel(1.0 / total_frames, first, *refs...]
  transfers between devices with their start and end apart: 5 -> 5, of which waited for: 3 -> 3; matrix products, arithmetic and copies ran while one was open for 0% -> 0% of each run, Pallas kernels for 16% -> 15%
where the time goes in v4:
time: 84.1 us; the launch traced here: 83.3 us
  blocking collectives  42.1 us (50%)
  Pallas kernels  16.8 us (20%)
  starting transfers between devices  12.4 us (15%)
  waiting for transfers between devices  10.1 us (12%)
  local copies, waits for them, and re-layouts  1.02 us (1%)
  between operations  0.88 us (1%)
    all_to_all x1, blocking collectives, on_device(): lax.all_to_all(outgoing, 'feed', split_axis=0, concat_axis=0, tiled=True)  42.1 us
    pallas_call x3, Pallas kernels, gram(): pl.pallas_call(lambda *refs: gram_kernel(1.0 / total_frames, first, *refs...  6.88 us
    ppermute x3, starting transfers between devices, on_device(): lax.ppermute(source[:, at * 128:(at + part) * 128], 'rep', swap)  6.51 us
    ppermute x3, waiting for transfers between devices, on_device(): lax.ppermute(source[:, at * 128:(at + part) * 128], 'rep', swap)  6.15 us
    ppermute x1, starting transfers between devices, on_device(): lax.ppermute(voltages[:, own_samples - (TAPS - 1) * DFT:], 'rep', [(0, 1)])  5.64 us
    pallas_call x1, Pallas kernels, beams(): pl.pallas_call(lambda *refs: beam_kernel(scale, *refs), out_shape=jax.Sha...  4.14 us
    ppermute x1, waiting for transfers between devices, on_device(): beam_other = lax.ppermute(beam_own, 'rep', swap)  3.96 us
    pallas_call x1, Pallas kernels, tap_blocks(): pl.pallas_call(lambda *refs: sums_kernel(chans, *refs), in_specs=[hbm] *...  3.1 us
  transfers between devices with their start and end apart: 5, of which 3 were waited for; matrix products, arithmetic and copies ran while one was open for 0% of the time, Pallas kernels for 15%

profile of v4, /device:TPU:1, one launch (start us, length us, event | category | flops | bytes accessed | tf_op | source)
XLA Modules:
  0.0 83.3 jit_solution(43375728252005231)
XLA Ops:
  0.6 0.9 %slice.12 = bf16[8,6144]{1,0:T(8,128)(2,1)S(1)} slice(bf16[8,131072]{1,0:T(8,128)(2,1)} %refs_0_.1), slice={[0:8], [124928:131072]} | slice | bytes 196608 | tf_op jit(solution)/shard_map/slice | solution.py:404
  1.5 5.6 %collective-permute-start = (bf16[8,6144]{1,0:T(8,128)(2,1)S(1)}, bf16[8,6144]{1,0:T(8,128)(2,1)S(1)}, u32[]{:S(2)}, u32[]{:S(2)}) collective-permute-start(bf16[8,6144]{1,0:T(8,128)(2,1)S(1)} %slice.12), channel_id=1, source_target_pairs={{0,1},{2,3},{4,5},{6,7},{8,9},{10,11},{12,13},{14,15},{16,17},{18,... | collective-permute-start | bytes 294920 | tf_op jit(solution)/shard_map/ppermute | solution.py:404
  7.2 3.1 %tap_sums.1 = (bf16[2,512,1024]{2,1,0:T(8,128)(2,1)S(1)}, bf16[512,512]{1,0:T(8,128)(2,1)S(1)}, bf16[8,8192]{1,0:T(8,128)(2,1)S(1)}, f32[1,8192]{1,0:T(1,128)S(1...) custom-call(bf16[8,131072]{1,0:T(8,128)(2,1)} %refs_0_.1, f32[1,8192]{1,0:T(1,128)} %bitcast.21, ...), custom_call_target="tpu_custom_call" | custom-call | flops 8388608 | bytes 8388608 | tf_op jit(solution)/shard_map/tap_sums/pallas_call | solution.py:195
  10.3 0.0 collective-permute-done.margin
  10.3 2.7 %spectra.1 = bf16[1024,512]{1,0:T(8,128)(2,1)S(1)} custom-call(bf16[2,512,1024]{2,1,0:T(8,128)(2,1)S(1)} %get-tuple-element.11.blocks, bf16[8,6144]{1,0:T(8,128)(2,1)S(1)} %collective-permute-done.margin, bf16[8,8192]{1,0:T(8,128)(2,1)S(1)} %get-tuple-element.12.head, f32[1,8192]{1,0:T(1,128)S(1)} %get-tuple-element.13.window, ...), custom_call_target="tpu_custom_call" | custom-call | flops 2147483648 | bytes 8388608 | tf_op jit(solution)/shard_map/spectra/pallas_call | solution.py:227
  13.0 0.0 copy-start
  13.0 0.0 copy-start.1
  13.0 42.1 %all_to_all.11 = bf16[128,8,512]{2,1,0:T(8,128)(2,1)S(1)} all-to-all(bf16[128,8,512]{2,1,0:T(8,128)(2,1)S(1)} %bitcast.18), channel_id=1, replica_groups=mesh['feed'=128,'rep'=2] {'feed'}, dimensions={0} | all-to-all | bytes 2097152 | tf_op jit(solution)/shard_map/all_to_all | solution.py:408
  55.1 3.4 %collective-permute-start.3 = (bf16[1024,256]{1,0:T(8,128)(2,1)S(1)}, bf16[1024,256]{1,0:T(8,128)(2,1)S(1)}, u32[]{:S(2)}, u32[]{:S(2)}) collective-permute-start(bf16[1024,256]{1,0:T(8,128)(2,1)S(1)} %slice.17), channel_id=1, source_target_pairs={{0,1},{1,0},{2,3},{3,2},{4,5},{5,4},{6,7},{7,6},{8,9},{9,8},{10,11... | collective-permute-start | bytes 1572872 | tf_op jit(solution)/shard_map/ppermute | solution.py:413
  58.5 0.1 collective-permute-start.2
  58.6 0.0 copy-done
  58.6 0.0 copy-done.1
  58.6 4.1 %beams.1.refs_4_ = f32[8,512]{1,0:T(8,128)S(1)} custom-call(bf16[1024,512]{1,0:T(8,128)(2,1)S(1)} %bitcast.13, s32[1,1024]{1,0:T(1,128)S(1)} %bitcast.19, bf16[256,128]{1,0:T(8,128)(2,1)S(1)} %copy-done.1), custom_call_target="tpu_custom_call" | custom-call | flops 2147483648 | bytes 4194304 | tf_op jit(solution)/shard_map/beams/pallas_call | solution.py:289
  62.8 3.0 %collective-permute-start.1 = (bf16[1024,128]{1,0:T(8,128)(2,1)S(1)}, bf16[1024,128]{1,0:T(8,128)(2,1)S(1)}, u32[]{:S(2)}, u32[]{:S(2)}) collective-permute-start(bf16[1024,128]{1,0:T(8,128)(2,1)S(1)} %slice.13), channel_id=1, source_target_pairs={{0,1},{1,0},{2,3},{3,2},{4,5},{5,4},{6,7},{7,6},{8,9},{9,8},{10,11... | collective-permute-start | bytes 786440 | tf_op jit(solution)/shard_map/ppermute | solution.py:413
  65.9 0.3 collective-permute-start.4
  66.1 3.4 %collective-permute-done.3.refs_2_ = bf16[1024,256]{1,0:T(8,128)(2,1)S(1)} collective-permute-done((bf16[1024,256]{1,0:T(8,128)(2,1)S(1)}, bf16[1024,256]{1,0:T(8,128)(2,1)S(1)}, u32[]{:S(2)}, u32[]{:S(2)}) %collective-permute-start.3) | collective-permute-done | bytes 524320 | tf_op jit(solution)/shard_map/ppermute | solution.py:413
  69.6 2.9 %gram.3.refs_3_ = bf16[256,8,16,128]{3,2,1,0:T(8,128)(2,1)} custom-call(s32[1]{0:T(128)} %bitcast.refs_0_, bf16[1024,512]{1,0:T(8,128)(2,1)S(1)} %bitcast.15, bf16[1024,256]{1,0:T(8,128)(2,1)S(1)} %collective-permute-done.3.refs_2_), custom_call_target="tpu_custom_call" | custom-call | flops 1073741824 | bytes 4194304 | tf_op jit(solution)/shard_map/gram/pallas_call | solution.py:376
  72.5 2.7 %collective-permute-done.2.refs_2_ = bf16[1024,128]{1,0:T(8,128)(2,1)S(1)} collective-permute-done((bf16[1024,128]{1,0:T(8,128)(2,1)S(1)}, bf16[1024,128]{1,0:T(8,128)(2,1)S(1)}, u32[]{:S(2)}, u32[]{:S(2)}) %collective-permute-start.2) | collective-permute-done | bytes 262176 | tf_op jit(solution)/shard_map/ppermute | solution.py:413
  75.2 2.0 %gram.4.refs_3_ = bf16[256,8,16,128]{3,2,1,0:T(8,128)(2,1)} custom-call(s32[1]{0:T(128)} %bitcast.refs_0_, bf16[1024,512]{1,0:T(8,128)(2,1)S(1)} %bitcast.16, bf16[1024,128]{1,0:T(8,128)(2,1)S(1)} %collective-permute-done.2.refs_2_, bf16[256,8,16,128]{3,2,1,0:T(8,128)(2,1)} %gram.3.refs_3_), custom_call_target="tpu_custom_call", output_to_operand_aliasing={{}: (3, {})} | custom-call | flops 536870912 | bytes 2097152 | tf_op jit(solution)/shard_map/gram/pallas_call | solution.py:376
  77.2 4.0 %collective-permute-done.4.refs_5_ = f32[8,512]{1,0:T(8,128)S(1)} collective-permute-done((f32[8,512]{1,0:T(8,128)S(1)}, f32[8,512]{1,0:T(8,128)S(1)}, u32[]{:S(2)}, u32[]{:S(2)}) %collective-permute-start.4) | collective-permute-done | bytes 16416 | tf_op jit(solution)/shard_map/ppermute | solution.py:415
  81.1 0.0 collective-permute-done.1.refs_2_
  81.1 2.0 %gram.5 = (bf16[256,8,16,128]{3,2,1,0:T(8,128)(2,1)}, f32[8,512]{1,0:T(8,128)}) custom-call(s32[1]{0:T(128)} %bitcast.refs_0_, bf16[1024,512]{1,0:T(8,128)(2,1)S(1)} %bitcast.17, bf16[1024,128]{1,0:T(8,128)(2,1)S(1)} %collective-permute-done.1.refs_2_, bf16[256,8,16,128]{3,2,1,0:T(8,128)(2,1)} %gram.4.refs_3_, ...), custom_call_target="tpu_custom_call", output_to_operand_aliasing={{0}: (3, {})} | custom-call | flops 536870912 | bytes 2097152 | tf_op jit(solution)/shard_map/gram/pallas_call | solution.py:376
  (3 shorter events, 0.1 us)
Async XLA Ops:
  1.5 8.8 %collective-permute-start = (bf16[8,6144]{1,0:T(8,128)(2,1)S(1)}, bf16[8,6144]{1,0:T(8,128)(2,1)S(1)}, u32[]{:S(2)}, u32[]{:S(2)}) collective-permute-start(bf16[8,6144]{1,0:T(8,128)(2,1)S(1)} %slice.12), channel_id=1, source_target_pairs={{0,1},{2,3},{4,5},{6,7},{8,9},{10,11},{12,13},{14,15},{16,17},{18,... | collective-permute-start | bytes 294920 | tf_op jit(solution)/shard_map/ppermute | solution.py:404
  13.0 45.6 %copy-start = (s32[1024]{0:T(1024)S(1)}, s32[1024]{0:T(1024)}, u32[]{:S(2)}) copy-start(s32[1024]{0:T(1024)} %param.9) | copy-start | bytes 12292
  13.0 45.6 %copy-start.1 = (bf16[256,128]{1,0:T(8,128)(2,1)S(1)}, bf16[256,128]{1,0:T(8,128)(2,1)}, u32[]{:S(2)}) copy-start(bf16[256,128]{1,0:T(8,128)(2,1)} %constant.9.clone.refs_2_) | copy-start | bytes 196612
  55.1 14.5 %collective-permute-start.3 = (bf16[1024,256]{1,0:T(8,128)(2,1)S(1)}, bf16[1024,256]{1,0:T(8,128)(2,1)S(1)}, u32[]{:S(2)}, u32[]{:S(2)}) collective-permute-start(bf16[1024,256]{1,0:T(8,128)(2,1)S(1)} %slice.17), channel_id=1, source_target_pairs={{0,1},{1,0},{2,3},{3,2},{4,5},{5,4},{6,7},{7,6},{8,9},{9,8},{10,11... | collective-permute-start | bytes 1572872 | tf_op jit(solution)/shard_map/ppermute | solution.py:413
  58.5 16.7 %collective-permute-start.2 = (bf16[1024,128]{1,0:T(8,128)(2,1)S(1)}, bf16[1024,128]{1,0:T(8,128)(2,1)S(1)}, u32[]{:S(2)}, u32[]{:S(2)}) collective-permute-start(bf16[1024,128]{1,0:T(8,128)(2,1)S(1)} %slice.16), channel_id=1, source_target_pairs={{0,1},{1,0},{2,3},{3,2},{4,5},{5,4},{6,7},{7,6},{8,9},{9,8},{10,11... | collective-permute-start | bytes 786440 | tf_op jit(solution)/shard_map/ppermute | solution.py:413
  62.8 18.3 %collective-permute-start.1 = (bf16[1024,128]{1,0:T(8,128)(2,1)S(1)}, bf16[1024,128]{1,0:T(8,128)(2,1)S(1)}, u32[]{:S(2)}, u32[]{:S(2)}) collective-permute-start(bf16[1024,128]{1,0:T(8,128)(2,1)S(1)} %slice.13), channel_id=1, source_target_pairs={{0,1},{1,0},{2,3},{3,2},{4,5},{5,4},{6,7},{7,6},{8,9},{9,8},{10,11... | collective-permute-start | bytes 786440 | tf_op jit(solution)/shard_map/ppermute | solution.py:413
  65.9 15.3 %collective-permute-start.4 = (f32[8,512]{1,0:T(8,128)S(1)}, f32[8,512]{1,0:T(8,128)S(1)}, u32[]{:S(2)}, u32[]{:S(2)}) collective-permute-start(f32[8,512]{1,0:T(8,128)S(1)} %beams.1.refs_4_), channel_id=1, source_target_pairs={{0,1},{1,0},{2,3},{3,2},{4,5},{5,4},{6,7},{7,6},{8,9},{9,8},{10,11... | collective-permute-start | bytes 49160 | tf_op jit(solution)/shard_map/ppermute | solution.py:415

commit v5 on v4

--- a/solution.py
+++ b/solution.py
@@ -316,7 +316,6 @@
     for c in range(other.shape[1] // 128):
         mine = pl.ds((first + c) * 128, 128)
         theirs = pl.ds(c * 128, 128)
-        left = []
         for half in range(2):
             start = pl.multiple_of(half * (inputs // 2) + rep[0] * count, count)
             plain, turned = [], []
@@ -324,24 +323,25 @@
                 plain.append(part)
                 swapped = pltpu.roll(part.astype(jnp.float32), 64, 1)
                 turned.append(jnp.where(lane < 64, swapped, -swapped).astype(jnp.bfloat16))
-            left += [jnp.concatenate(plain, axis=1), jnp.concatenate(turned, axis=1)]
-        left = jnp.concatenate(left, axis=0)
-        for at in range(0, inputs, 256):
-            right = jnp.concatenate([own[at : at + 256, mine], other[at : at + 256, theirs]], axis=1)
-            products = lax.dot_general(left, right, NT, preferred_element_type=jnp.float32)
-            for half in range(2):
+            left = jnp.concatenate(
+                [jnp.concatenate(plain, axis=1), jnp.concatenate(turned, axis=1)], axis=0
+            )
+            base = half * count * pitch
+            for at in range(0, inputs, 256):
+                right = jnp.concatenate(
+                    [own[at : at + 256, mine], other[at : at + 256, theirs]], axis=1
+                )
+                products = lax.dot_general(left, right, NT, preferred_element_type=jnp.float32)
                 for part in range(2):
                     for tile in range(2):
-                        to = half * count * pitch + (at // 128 + tile) * 2 + part
-                        row = (2 * half + part) * count
+                        to = base + (at // 128 + tile) * 2 + part
                         rows[pl.ds(to, count, stride=pitch), :] = products[
-                            row : row + count, tile * 128 : (tile + 1) * 128
+                            part * count : (part + 1) * count, tile * 128 : (tile + 1) * 128
                         ]
-        for half in range(2):
             slot = 2 * c + half
             for piece in range(0, count, PIECE):
                 for r in range(piece, piece + PIECE):
-                    at = (half * count + r) * pitch
+                    at = base + r * pitch
                     stage[slot, r] = (rows[at : at + tiles, :] * scale).astype(jnp.bfloat16)
                 copies.append(
                     pltpu.make_async_copy(

time: 84.1 us -> 84.1 us (level)
  no operation moved by 1% of the time
where the time goes in v5:
time: 84.1 us; the launch traced here: 83.3 us
  blocking collectives  42.1 us (50%)
  Pallas kernels  16.7 us (20%)
  starting transfers between devices  12.4 us (15%)
  waiting for transfers between devices  10.1 us (12%)
  local copies, waits for them, and re-layouts  1.02 us (1%)
  between operations  0.88 us (1%)
    all_to_all x1, blocking collectives, on_device(): lax.all_to_all(outgoing, 'feed', split_axis=0, concat_axis=0, tiled=True)  42.1 us
    pallas_call x3, Pallas kernels, gram(): pl.pallas_call(lambda *refs: gram_kernel(1.0 / total_frames, first, *refs...  6.81 us
    ppermute x3, starting transfers between devices, on_device(): lax.ppermute(source[:, at * 128:(at + part) * 128], 'rep', swap)  6.51 us
    ppermute x3, waiting for transfers between devices, on_device(): lax.ppermute(source[:, at * 128:(at + part) * 128], 'rep', swap)  6.11 us
    ppermute x1, starting transfers between devices, on_device(): lax.ppermute(voltages[:, own_samples - (TAPS - 1) * DFT:], 'rep', [(0, 1)])  5.64 us
    pallas_call x1, Pallas kernels, beams(): pl.pallas_call(lambda *refs: beam_kernel(scale, *refs), out_shape=jax.Sha...  4.14 us
    ppermute x1, waiting for transfers between devices, on_device(): beam_other = lax.ppermute(beam_own, 'rep', swap)  4.01 us
    pallas_call x1, Pallas kernels, tap_blocks(): pl.pallas_call(lambda *refs: sums_kernel(chans, *refs), in_specs=[hbm] *...  3.1 us
  transfers between devices with their start and end apart: 5, of which 3 were waited for; matrix products, arithmetic and copies ran while one was open for 0% of the time, Pallas kernels for 15%

profile of v5, /device:TPU:1, one launch (start us, length us, event | category | flops | bytes accessed | tf_op | source)
XLA Modules:
  0.0 83.3 jit_solution(14516311337115857457)
XLA Ops:
  0.6 0.9 %slice.12 = bf16[8,6144]{1,0:T(8,128)(2,1)S(1)} slice(bf16[8,131072]{1,0:T(8,128)(2,1)} %refs_0_.1), slice={[0:8], [124928:131072]} | slice | bytes 196608 | tf_op jit(solution)/shard_map/slice | solution.py:404
  1.5 5.6 %collective-permute-start = (bf16[8,6144]{1,0:T(8,128)(2,1)S(1)}, bf16[8,6144]{1,0:T(8,128)(2,1)S(1)}, u32[]{:S(2)}, u32[]{:S(2)}) collective-permute-start(bf16[8,6144]{1,0:T(8,128)(2,1)S(1)} %slice.12), channel_id=1, source_target_pairs={{0,1},{2,3},{4,5},{6,7},{8,9},{10,11},{12,13},{14,15},{16,17},{18,... | collective-permute-start | bytes 294920 | tf_op jit(solution)/shard_map/ppermute | solution.py:404
  7.2 3.1 %tap_sums.1 = (bf16[2,512,1024]{2,1,0:T(8,128)(2,1)S(1)}, bf16[512,512]{1,0:T(8,128)(2,1)S(1)}, bf16[8,8192]{1,0:T(8,128)(2,1)S(1)}, f32[1,8192]{1,0:T(1,128)S(1...) custom-call(bf16[8,131072]{1,0:T(8,128)(2,1)} %refs_0_.1, f32[1,8192]{1,0:T(1,128)} %bitcast.21, ...), custom_call_target="tpu_custom_call" | custom-call | flops 8388608 | bytes 8388608 | tf_op jit(solution)/shard_map/tap_sums/pallas_call | solution.py:195
  10.3 0.0 collective-permute-done.margin
  10.3 2.7 %spectra.1 = bf16[1024,512]{1,0:T(8,128)(2,1)S(1)} custom-call(bf16[2,512,1024]{2,1,0:T(8,128)(2,1)S(1)} %get-tuple-element.11.blocks, bf16[8,6144]{1,0:T(8,128)(2,1)S(1)} %collective-permute-done.margin, bf16[8,8192]{1,0:T(8,128)(2,1)S(1)} %get-tuple-element.12.head, f32[1,8192]{1,0:T(1,128)S(1)} %get-tuple-element.13.window, ...), custom_call_target="tpu_custom_call" | custom-call | flops 2147483648 | bytes 8388608 | tf_op jit(solution)/shard_map/spectra/pallas_call | solution.py:227
  13.0 0.0 copy-start
  13.0 0.0 copy-start.1
  13.0 42.1 %all_to_all.11 = bf16[128,8,512]{2,1,0:T(8,128)(2,1)S(1)} all-to-all(bf16[128,8,512]{2,1,0:T(8,128)(2,1)S(1)} %bitcast.18), channel_id=1, replica_groups=mesh['feed'=128,'rep'=2] {'feed'}, dimensions={0} | all-to-all | bytes 2097152 | tf_op jit(solution)/shard_map/all_to_all | solution.py:408
  55.1 3.4 %collective-permute-start.3 = (bf16[1024,256]{1,0:T(8,128)(2,1)S(1)}, bf16[1024,256]{1,0:T(8,128)(2,1)S(1)}, u32[]{:S(2)}, u32[]{:S(2)}) collective-permute-start(bf16[1024,256]{1,0:T(8,128)(2,1)S(1)} %slice.17), channel_id=1, source_target_pairs={{0,1},{1,0},{2,3},{3,2},{4,5},{5,4},{6,7},{7,6},{8,9},{9,8},{10,11... | collective-permute-start | bytes 1572872 | tf_op jit(solution)/shard_map/ppermute | solution.py:413
  58.5 0.1 collective-permute-start.2
  58.6 0.0 copy-done
  58.6 0.0 copy-done.1
  58.6 4.1 %beams.1.refs_4_ = f32[8,512]{1,0:T(8,128)S(1)} custom-call(bf16[1024,512]{1,0:T(8,128)(2,1)S(1)} %bitcast.13, s32[1,1024]{1,0:T(1,128)S(1)} %bitcast.19, bf16[256,128]{1,0:T(8,128)(2,1)S(1)} %copy-done.1), custom_call_target="tpu_custom_call" | custom-call | flops 2147483648 | bytes 4194304 | tf_op jit(solution)/shard_map/beams/pallas_call | solution.py:289
  62.8 3.0 %collective-permute-start.1 = (bf16[1024,128]{1,0:T(8,128)(2,1)S(1)}, bf16[1024,128]{1,0:T(8,128)(2,1)S(1)}, u32[]{:S(2)}, u32[]{:S(2)}) collective-permute-start(bf16[1024,128]{1,0:T(8,128)(2,1)S(1)} %slice.13), channel_id=1, source_target_pairs={{0,1},{1,0},{2,3},{3,2},{4,5},{5,4},{6,7},{7,6},{8,9},{9,8},{10,11... | collective-permute-start | bytes 786440 | tf_op jit(solution)/shard_map/ppermute | solution.py:413
  65.9 0.3 collective-permute-start.4
  66.1 3.4 %collective-permute-done.3.refs_2_ = bf16[1024,256]{1,0:T(8,128)(2,1)S(1)} collective-permute-done((bf16[1024,256]{1,0:T(8,128)(2,1)S(1)}, bf16[1024,256]{1,0:T(8,128)(2,1)S(1)}, u32[]{:S(2)}, u32[]{:S(2)}) %collective-permute-start.3) | collective-permute-done | bytes 524320 | tf_op jit(solution)/shard_map/ppermute | solution.py:413
  69.6 2.9 %gram.3.refs_3_ = bf16[256,8,16,128]{3,2,1,0:T(8,128)(2,1)} custom-call(s32[1]{0:T(128)} %bitcast.refs_0_, bf16[1024,512]{1,0:T(8,128)(2,1)S(1)} %bitcast.15, bf16[1024,256]{1,0:T(8,128)(2,1)S(1)} %collective-permute-done.3.refs_2_), custom_call_target="tpu_custom_call" | custom-call | flops 1073741824 | bytes 4194304 | tf_op jit(solution)/shard_map/gram/pallas_call | solution.py:376
  72.5 2.7 %collective-permute-done.2.refs_2_ = bf16[1024,128]{1,0:T(8,128)(2,1)S(1)} collective-permute-done((bf16[1024,128]{1,0:T(8,128)(2,1)S(1)}, bf16[1024,128]{1,0:T(8,128)(2,1)S(1)}, u32[]{:S(2)}, u32[]{:S(2)}) %collective-permute-start.2) | collective-permute-done | bytes 262176 | tf_op jit(solution)/shard_map/ppermute | solution.py:413
  75.2 1.9 %gram.4.refs_3_ = bf16[256,8,16,128]{3,2,1,0:T(8,128)(2,1)} custom-call(s32[1]{0:T(128)} %bitcast.refs_0_, bf16[1024,512]{1,0:T(8,128)(2,1)S(1)} %bitcast.16, bf16[1024,128]{1,0:T(8,128)(2,1)S(1)} %collective-permute-done.2.refs_2_, bf16[256,8,16,128]{3,2,1,0:T(8,128)(2,1)} %gram.3.refs_3_), custom_call_target="tpu_custom_call", output_to_operand_aliasing={{}: (3, {})} | custom-call | flops 536870912 | bytes 2097152 | tf_op jit(solution)/shard_map/gram/pallas_call | solution.py:376
  77.1 4.0 %collective-permute-done.4.refs_5_ = f32[8,512]{1,0:T(8,128)S(1)} collective-permute-done((f32[8,512]{1,0:T(8,128)S(1)}, f32[8,512]{1,0:T(8,128)S(1)}, u32[]{:S(2)}, u32[]{:S(2)}) %collective-permute-start.4) | collective-permute-done | bytes 16416 | tf_op jit(solution)/shard_map/ppermute | solution.py:415
  81.1 0.0 collective-permute-done.1.refs_2_
  81.1 1.9 %gram.5 = (bf16[256,8,16,128]{3,2,1,0:T(8,128)(2,1)}, f32[8,512]{1,0:T(8,128)}) custom-call(s32[1]{0:T(128)} %bitcast.refs_0_, bf16[1024,512]{1,0:T(8,128)(2,1)S(1)} %bitcast.17, bf16[1024,128]{1,0:T(8,128)(2,1)S(1)} %collective-permute-done.1.refs_2_, bf16[256,8,16,128]{3,2,1,0:T(8,128)(2,1)} %gram.4.refs_3_, ...), custom_call_target="tpu_custom_call", output_to_operand_aliasing={{0}: (3, {})} | custom-call | flops 536870912 | bytes 2097152 | tf_op jit(solution)/shard_map/gram/pallas_call | solution.py:376
  (3 shorter events, 0.1 us)
Async XLA Ops:
  1.5 8.8 %collective-permute-start = (bf16[8,6144]{1,0:T(8,128)(2,1)S(1)}, bf16[8,6144]{1,0:T(8,128)(2,1)S(1)}, u32[]{:S(2)}, u32[]{:S(2)}) collective-permute-start(bf16[8,6144]{1,0:T(8,128)(2,1)S(1)} %slice.12), channel_id=1, source_target_pairs={{0,1},{2,3},{4,5},{6,7},{8,9},{10,11},{12,13},{14,15},{16,17},{18,... | collective-permute-start | bytes 294920 | tf_op jit(solution)/shard_map/ppermute | solution.py:404
  13.0 45.6 %copy-start = (s32[1024]{0:T(1024)S(1)}, s32[1024]{0:T(1024)}, u32[]{:S(2)}) copy-start(s32[1024]{0:T(1024)} %param.9) | copy-start | bytes 12292
  13.0 45.6 %copy-start.1 = (bf16[256,128]{1,0:T(8,128)(2,1)S(1)}, bf16[256,128]{1,0:T(8,128)(2,1)}, u32[]{:S(2)}) copy-start(bf16[256,128]{1,0:T(8,128)(2,1)} %constant.9.clone.refs_2_) | copy-start | bytes 196612
  55.1 14.5 %collective-permute-start.3 = (bf16[1024,256]{1,0:T(8,128)(2,1)S(1)}, bf16[1024,256]{1,0:T(8,128)(2,1)S(1)}, u32[]{:S(2)}, u32[]{:S(2)}) collective-permute-start(bf16[1024,256]{1,0:T(8,128)(2,1)S(1)} %slice.17), channel_id=1, source_target_pairs={{0,1},{1,0},{2,3},{3,2},{4,5},{5,4},{6,7},{7,6},{8,9},{9,8},{10,11... | collective-permute-start | bytes 1572872 | tf_op jit(solution)/shard_map/ppermute | solution.py:413
  58.5 16.7 %collective-permute-start.2 = (bf16[1024,128]{1,0:T(8,128)(2,1)S(1)}, bf16[1024,128]{1,0:T(8,128)(2,1)S(1)}, u32[]{:S(2)}, u32[]{:S(2)}) collective-permute-start(bf16[1024,128]{1,0:T(8,128)(2,1)S(1)} %slice.16), channel_id=1, source_target_pairs={{0,1},{1,0},{2,3},{3,2},{4,5},{5,4},{6,7},{7,6},{8,9},{9,8},{10,11... | collective-permute-start | bytes 786440 | tf_op jit(solution)/shard_map/ppermute | solution.py:413
  62.8 18.3 %collective-permute-start.1 = (bf16[1024,128]{1,0:T(8,128)(2,1)S(1)}, bf16[1024,128]{1,0:T(8,128)(2,1)S(1)}, u32[]{:S(2)}, u32[]{:S(2)}) collective-permute-start(bf16[1024,128]{1,0:T(8,128)(2,1)S(1)} %slice.13), channel_id=1, source_target_pairs={{0,1},{1,0},{2,3},{3,2},{4,5},{5,4},{6,7},{7,6},{8,9},{9,8},{10,11... | collective-permute-start | bytes 786440 | tf_op jit(solution)/shard_map/ppermute | solution.py:413
  65.9 15.3 %collective-permute-start.4 = (f32[8,512]{1,0:T(8,128)S(1)}, f32[8,512]{1,0:T(8,128)S(1)}, u32[]{:S(2)}, u32[]{:S(2)}) collective-permute-start(f32[8,512]{1,0:T(8,128)S(1)} %beams.1.refs_4_), channel_id=1, source_target_pairs={{0,1},{1,0},{2,3},{3,2},{4,5},{5,4},{6,7},{7,6},{8,9},{9,8},{10,11... | collective-permute-start | bytes 49160 | tf_op jit(solution)/shard_map/ppermute | solution.py:415

commit v6 on v5

--- a/solution.py
+++ b/solution.py
@@ -153,15 +153,16 @@
             sums, waves[parity], preferred_element_type=jnp.float32
         ).astype(jnp.bfloat16)
     for parity in range(2):
+        turned = jnp.dot(
+            order[...],
+            spectra[:, parity * CHANNELS : (parity + 1) * CHANNELS],
+            preferred_element_type=jnp.float32,
+        ).astype(jnp.bfloat16)
         for part in range(2):
-            at = parity * CHANNELS + part * half_ch
-            turned = jnp.dot(
-                order[...], spectra[:, at : at + half_ch], preferred_element_type=jnp.float32
-            ).astype(jnp.bfloat16)
             for i in range(inputs):
                 to = (2 * i + part) * frames
                 sorted_[to : to + frames, parity * half_ch : (parity + 1) * half_ch] = turned[
-                    i * frames : (i + 1) * frames, :
+                    i * frames : (i + 1) * frames, part * half_ch : (part + 1) * half_ch
                 ]
     wide = 2 * frames
     pitch = inputs + 1

time: 84.1 us -> 84.1 us (level)
  no operation moved by 1% of the time
where the time goes in v6:
time: 84.1 us; the launch traced here: 83.3 us
  blocking collectives  42.1 us (50%)
  Pallas kernels  16.7 us (20%)
  starting transfers between devices  12.4 us (15%)
  waiting for transfers between devices  10.1 us (12%)
  local copies, waits for them, and re-layouts  1.02 us (1%)
  between operations  0.88 us (1%)
    all_to_all x1, blocking collectives, on_device(): lax.all_to_all(outgoing, 'feed', split_axis=0, concat_axis=0, tiled=True)  42.1 us
    pallas_call x3, Pallas kernels, gram(): pl.pallas_call(lambda *refs: gram_kernel(1.0 / total_frames, first, *refs...  6.81 us
    ppermute x3, starting transfers between devices, on_device(): lax.ppermute(source[:, at * 128:(at + part) * 128], 'rep', swap)  6.51 us
    ppermute x3, waiting for transfers between devices, on_device(): lax.ppermute(source[:, at * 128:(at + part) * 128], 'rep', swap)  6.11 us
    ppermute x1, starting transfers between devices, on_device(): lax.ppermute(voltages[:, own_samples - (TAPS - 1) * DFT:], 'rep', [(0, 1)])  5.64 us
    pallas_call x1, Pallas kernels, beams(): pl.pallas_call(lambda *refs: beam_kernel(scale, *refs), out_shape=jax.Sha...  4.14 us
    ppermute x1, waiting for transfers between devices, on_device(): beam_other = lax.ppermute(beam_own, 'rep', swap)  4.01 us
    pallas_call x1, Pallas kernels, tap_blocks(): pl.pallas_call(lambda *refs: sums_kernel(chans, *refs), in_specs=[hbm] *...  3.1 us
  transfers between devices with their start and end apart: 5, of which 3 were waited for; matrix products, arithmetic and copies ran while one was open for 0% of the time, Pallas kernels for 15%

profile of v6, /device:TPU:1, one launch (start us, length us, event | category | flops | bytes accessed | tf_op | source)
XLA Modules:
  0.0 83.3 jit_solution(14516311337115857457)
XLA Ops:
  0.6 0.9 %slice.12 = bf16[8,6144]{1,0:T(8,128)(2,1)S(1)} slice(bf16[8,131072]{1,0:T(8,128)(2,1)} %refs_0_.1), slice={[0:8], [124928:131072]} | slice | bytes 196608 | tf_op jit(solution)/shard_map/slice | solution.py:405
  1.5 5.6 %collective-permute-start = (bf16[8,6144]{1,0:T(8,128)(2,1)S(1)}, bf16[8,6144]{1,0:T(8,128)(2,1)S(1)}, u32[]{:S(2)}, u32[]{:S(2)}) collective-permute-start(bf16[8,6144]{1,0:T(8,128)(2,1)S(1)} %slice.12), channel_id=1, source_target_pairs={{0,1},{2,3},{4,5},{6,7},{8,9},{10,11},{12,13},{14,15},{16,17},{18,... | collective-permute-start | bytes 294920 | tf_op jit(solution)/shard_map/ppermute | solution.py:405
  7.2 3.1 %tap_sums.1 = (bf16[2,512,1024]{2,1,0:T(8,128)(2,1)S(1)}, bf16[512,512]{1,0:T(8,128)(2,1)S(1)}, bf16[8,8192]{1,0:T(8,128)(2,1)S(1)}, f32[1,8192]{1,0:T(1,128)S(1...) custom-call(bf16[8,131072]{1,0:T(8,128)(2,1)} %refs_0_.1, f32[1,8192]{1,0:T(1,128)} %bitcast.21, ...), custom_call_target="tpu_custom_call" | custom-call | flops 8388608 | bytes 8388608 | tf_op jit(solution)/shard_map/tap_sums/pallas_call | solution.py:196
  10.3 0.0 collective-permute-done.margin
  10.3 2.7 %spectra.1 = bf16[1024,512]{1,0:T(8,128)(2,1)S(1)} custom-call(bf16[2,512,1024]{2,1,0:T(8,128)(2,1)S(1)} %get-tuple-element.11.blocks, bf16[8,6144]{1,0:T(8,128)(2,1)S(1)} %collective-permute-done.margin, bf16[8,8192]{1,0:T(8,128)(2,1)S(1)} %get-tuple-element.12.head, f32[1,8192]{1,0:T(1,128)S(1)} %get-tuple-element.13.window, ...), custom_call_target="tpu_custom_call" | custom-call | flops 2147483648 | bytes 8388608 | tf_op jit(solution)/shard_map/spectra/pallas_call | solution.py:228
  13.0 0.0 copy-start
  13.0 0.0 copy-start.1
  13.0 42.1 %all_to_all.11 = bf16[128,8,512]{2,1,0:T(8,128)(2,1)S(1)} all-to-all(bf16[128,8,512]{2,1,0:T(8,128)(2,1)S(1)} %bitcast.18), channel_id=1, replica_groups=mesh['feed'=128,'rep'=2] {'feed'}, dimensions={0} | all-to-all | bytes 2097152 | tf_op jit(solution)/shard_map/all_to_all | solution.py:409
  55.1 3.4 %collective-permute-start.3 = (bf16[1024,256]{1,0:T(8,128)(2,1)S(1)}, bf16[1024,256]{1,0:T(8,128)(2,1)S(1)}, u32[]{:S(2)}, u32[]{:S(2)}) collective-permute-start(bf16[1024,256]{1,0:T(8,128)(2,1)S(1)} %slice.17), channel_id=1, source_target_pairs={{0,1},{1,0},{2,3},{3,2},{4,5},{5,4},{6,7},{7,6},{8,9},{9,8},{10,11... | collective-permute-start | bytes 1572872 | tf_op jit(solution)/shard_map/ppermute | solution.py:414
  58.5 0.1 collective-permute-start.2
  58.6 0.0 copy-done
  58.6 0.0 copy-done.1
  58.6 4.1 %beams.1.refs_4_ = f32[8,512]{1,0:T(8,128)S(1)} custom-call(bf16[1024,512]{1,0:T(8,128)(2,1)S(1)} %bitcast.13, s32[1,1024]{1,0:T(1,128)S(1)} %bitcast.19, bf16[256,128]{1,0:T(8,128)(2,1)S(1)} %copy-done.1), custom_call_target="tpu_custom_call" | custom-call | flops 2147483648 | bytes 4194304 | tf_op jit(solution)/shard_map/beams/pallas_call | solution.py:290
  62.8 3.0 %collective-permute-start.1 = (bf16[1024,128]{1,0:T(8,128)(2,1)S(1)}, bf16[1024,128]{1,0:T(8,128)(2,1)S(1)}, u32[]{:S(2)}, u32[]{:S(2)}) collective-permute-start(bf16[1024,128]{1,0:T(8,128)(2,1)S(1)} %slice.13), channel_id=1, source_target_pairs={{0,1},{1,0},{2,3},{3,2},{4,5},{5,4},{6,7},{7,6},{8,9},{9,8},{10,11... | collective-permute-start | bytes 786440 | tf_op jit(solution)/shard_map/ppermute | solution.py:414
  65.9 0.3 collective-permute-start.4
  66.1 3.4 %collective-permute-done.3.refs_2_ = bf16[1024,256]{1,0:T(8,128)(2,1)S(1)} collective-permute-done((bf16[1024,256]{1,0:T(8,128)(2,1)S(1)}, bf16[1024,256]{1,0:T(8,128)(2,1)S(1)}, u32[]{:S(2)}, u32[]{:S(2)}) %collective-permute-start.3) | collective-permute-done | bytes 524320 | tf_op jit(solution)/shard_map/ppermute | solution.py:414
  69.6 2.9 %gram.3.refs_3_ = bf16[256,8,16,128]{3,2,1,0:T(8,128)(2,1)} custom-call(s32[1]{0:T(128)} %bitcast.refs_0_, bf16[1024,512]{1,0:T(8,128)(2,1)S(1)} %bitcast.15, bf16[1024,256]{1,0:T(8,128)(2,1)S(1)} %collective-permute-done.3.refs_2_), custom_call_target="tpu_custom_call" | custom-call | flops 1073741824 | bytes 4194304 | tf_op jit(solution)/shard_map/gram/pallas_call | solution.py:377
  72.5 2.7 %collective-permute-done.2.refs_2_ = bf16[1024,128]{1,0:T(8,128)(2,1)S(1)} collective-permute-done((bf16[1024,128]{1,0:T(8,128)(2,1)S(1)}, bf16[1024,128]{1,0:T(8,128)(2,1)S(1)}, u32[]{:S(2)}, u32[]{:S(2)}) %collective-permute-start.2) | collective-permute-done | bytes 262176 | tf_op jit(solution)/shard_map/ppermute | solution.py:414
  75.2 1.9 %gram.4.refs_3_ = bf16[256,8,16,128]{3,2,1,0:T(8,128)(2,1)} custom-call(s32[1]{0:T(128)} %bitcast.refs_0_, bf16[1024,512]{1,0:T(8,128)(2,1)S(1)} %bitcast.16, bf16[1024,128]{1,0:T(8,128)(2,1)S(1)} %collective-permute-done.2.refs_2_, bf16[256,8,16,128]{3,2,1,0:T(8,128)(2,1)} %gram.3.refs_3_), custom_call_target="tpu_custom_call", output_to_operand_aliasing={{}: (3, {})} | custom-call | flops 536870912 | bytes 2097152 | tf_op jit(solution)/shard_map/gram/pallas_call | solution.py:377
  77.1 4.0 %collective-permute-done.4.refs_5_ = f32[8,512]{1,0:T(8,128)S(1)} collective-permute-done((f32[8,512]{1,0:T(8,128)S(1)}, f32[8,512]{1,0:T(8,128)S(1)}, u32[]{:S(2)}, u32[]{:S(2)}) %collective-permute-start.4) | collective-permute-done | bytes 16416 | tf_op jit(solution)/shard_map/ppermute | solution.py:416
  81.1 0.0 collective-permute-done.1.refs_2_
  81.1 1.9 %gram.5 = (bf16[256,8,16,128]{3,2,1,0:T(8,128)(2,1)}, f32[8,512]{1,0:T(8,128)}) custom-call(s32[1]{0:T(128)} %bitcast.refs_0_, bf16[1024,512]{1,0:T(8,128)(2,1)S(1)} %bitcast.17, bf16[1024,128]{1,0:T(8,128)(2,1)S(1)} %collective-permute-done.1.refs_2_, bf16[256,8,16,128]{3,2,1,0:T(8,128)(2,1)} %gram.4.refs_3_, ...), custom_call_target="tpu_custom_call", output_to_operand_aliasing={{0}: (3, {})} | custom-call | flops 536870912 | bytes 2097152 | tf_op jit(solution)/shard_map/gram/pallas_call | solution.py:377
  (3 shorter events, 0.1 us)
Async XLA Ops:
  1.5 8.8 %collective-permute-start = (bf16[8,6144]{1,0:T(8,128)(2,1)S(1)}, bf16[8,6144]{1,0:T(8,128)(2,1)S(1)}, u32[]{:S(2)}, u32[]{:S(2)}) collective-permute-start(bf16[8,6144]{1,0:T(8,128)(2,1)S(1)} %slice.12), channel_id=1, source_target_pairs={{0,1},{2,3},{4,5},{6,7},{8,9},{10,11},{12,13},{14,15},{16,17},{18,... | collective-permute-start | bytes 294920 | tf_op jit(solution)/shard_map/ppermute | solution.py:405
  13.0 45.6 %copy-start = (s32[1024]{0:T(1024)S(1)}, s32[1024]{0:T(1024)}, u32[]{:S(2)}) copy-start(s32[1024]{0:T(1024)} %param.9) | copy-start | bytes 12292
  13.0 45.6 %copy-start.1 = (bf16[256,128]{1,0:T(8,128)(2,1)S(1)}, bf16[256,128]{1,0:T(8,128)(2,1)}, u32[]{:S(2)}) copy-start(bf16[256,128]{1,0:T(8,128)(2,1)} %constant.9.clone.refs_2_) | copy-start | bytes 196612
  55.1 14.5 %collective-permute-start.3 = (bf16[1024,256]{1,0:T(8,128)(2,1)S(1)}, bf16[1024,256]{1,0:T(8,128)(2,1)S(1)}, u32[]{:S(2)}, u32[]{:S(2)}) collective-permute-start(bf16[1024,256]{1,0:T(8,128)(2,1)S(1)} %slice.17), channel_id=1, source_target_pairs={{0,1},{1,0},{2,3},{3,2},{4,5},{5,4},{6,7},{7,6},{8,9},{9,8},{10,11... | collective-permute-start | bytes 1572872 | tf_op jit(solution)/shard_map/ppermute | solution.py:414
  58.5 16.7 %collective-permute-start.2 = (bf16[1024,128]{1,0:T(8,128)(2,1)S(1)}, bf16[1024,128]{1,0:T(8,128)(2,1)S(1)}, u32[]{:S(2)}, u32[]{:S(2)}) collective-permute-start(bf16[1024,128]{1,0:T(8,128)(2,1)S(1)} %slice.16), channel_id=1, source_target_pairs={{0,1},{1,0},{2,3},{3,2},{4,5},{5,4},{6,7},{7,6},{8,9},{9,8},{10,11... | collective-permute-start | bytes 786440 | tf_op jit(solution)/shard_map/ppermute | solution.py:414
  62.8 18.3 %collective-permute-start.1 = (bf16[1024,128]{1,0:T(8,128)(2,1)S(1)}, bf16[1024,128]{1,0:T(8,128)(2,1)S(1)}, u32[]{:S(2)}, u32[]{:S(2)}) collective-permute-start(bf16[1024,128]{1,0:T(8,128)(2,1)S(1)} %slice.13), channel_id=1, source_target_pairs={{0,1},{1,0},{2,3},{3,2},{4,5},{5,4},{6,7},{7,6},{8,9},{9,8},{10,11... | collective-permute-start | bytes 786440 | tf_op jit(solution)/shard_map/ppermute | solution.py:414
  65.9 15.3 %collective-permute-start.4 = (f32[8,512]{1,0:T(8,128)S(1)}, f32[8,512]{1,0:T(8,128)S(1)}, u32[]{:S(2)}, u32[]{:S(2)}) collective-permute-start(f32[8,512]{1,0:T(8,128)S(1)} %beams.1.refs_4_), channel_id=1, source_target_pairs={{0,1},{1,0},{2,3},{3,2},{4,5},{5,4},{6,7},{7,6},{8,9},{9,8},{10,11... | collective-permute-start | bytes 49160 | tf_op jit(solution)/shard_map/ppermute | solution.py:416
